TPU v7x, 32 devices: a whole 2x2x4 slice. The times are simulated.
32 devices in a mesh: groups: 2 (over x), dp: 8 (over z, y), tensor: 2 (over core).
Axes of the slice: x: 2, y: 2, z: 4, core: 2. Of those that a mesh axis runs over, the one named last changes fastest.
Arguments:
- activations: bfloat16 [4096, 28672], P(('groups', 'dp'), 'tensor'), parts along dimension 0, may hold values from -6 to 6
- out_grads: bfloat16 [4096, 8192], P(('groups', 'dp'), 'tensor'), parts along dimension 0, may hold values from -6 to 6
- proj_in: bfloat16 [28672, 64], P('tensor'), may hold values from -0.03125 to 0.03125
- proj_out: bfloat16 [8192, 64], P('tensor'), may hold values from -0.0625 to 0.0625
- stored: bfloat16 [16384, 4096], P(('groups', 'dp')), parts along dimension 0, may hold values from -0.375 to 0.375
- counts: int32 [256], P(('groups', 'dp')), parts along dimension 0, may hold values from 1 to 16
- query_ids: int32 [512], P('groups'), parts along dimension 0, may hold values from 0 to 127
Outputs:
- gram: float32 [8192, 4096], P(('groups', 'dp'), 'tensor'), parts along dimension 0
- scores: float32 [512, 128], P('groups', 'dp'), parts along dimension 0
There are 2 independent parts, one for each index of `groups`. A program takes and returns all parts, laid end to end along the dimension named above; an argument that names none is the same for every part. Nothing has to cross between parts.
All inputs are finite; a program needn't handle non-finite values.
Results may differ from a plain program's by a relative error of at most 0.015.
Values may be sent and summed in bfloat16 or wider, within the bound.
No kernel may reach another device: no remote copies, remote signals or barrier semaphores. Data moves between devices by JAX's collectives and lax.ppermute only.
A program may use at most 192 MiB of HBM per device.

v0:
```python
import jax
import jax.numpy as jnp
from jax import lax
from jax.experimental import pallas as pl
from jax.experimental.pallas import tpu as pltpu
from jax.sharding import PartitionSpec as P

R = 64
SEQ = 16
damping = 1.0
EXACT = lax.Precision.HIGHEST
SWAP = [(0, 1), (1, 0)]
VMEM_BYTES = 56 * 1024 * 1024
SMALL_BYTES = 12 * 1024 * 1024
LIGHT = pl.CostEstimate(flops=10**6, bytes_accessed=10**5, transcendentals=0)
ANYWHERE = pl.BlockSpec(memory_space=pl.ANY)
MAIN = pl.BlockSpec(memory_space=pltpu.HBM)
FAST = pl.BlockSpec(memory_space=pltpu.VMEM)


class Ring:
    def __init__(self, mesh):
        self.count = mesh.shape["dp"]
        self.half = self.count // 2
        coords = [getattr(device, "coords", None) for device in mesh.devices[0, :, 0]]
        self.folded = False
        if None not in coords:
            moving = [axis for axis in range(3) if len({place[axis] for place in coords}) > 1]
            fast = [axis for axis in moving if coords[0][axis] != coords[1][axis]]
            self.folded = len(moving) == 2 and len(fast) == 1 and len({place[fast[0]] for place in coords}) == 2
        reach = [0, 0]
        self.offsets = []
        for distance in range(self.half - 1, 0, -1):
            side = 0 if reach[0] <= reach[1] else 1
            reach[side] += distance
            self.offsets.append(distance if side == 0 else -distance)

    def index_at(self, position):
        if isinstance(position, int):
            position = position % self.count
            if not self.folded:
                return position
            return 2 * position if position < self.half else 2 * (self.count - 1 - position) + 1
        position = lax.rem(position + 2 * self.count, self.count)
        if not self.folded:
            return position
        return jnp.where(position < self.half, 2 * position, 2 * (self.count - 1 - position) + 1)

    def position_of(self, index):
        if not self.folded:
            return index
        return jnp.where(lax.rem(index, 2) == 0, index // 2, self.count - 1 - index // 2)

    def shift(self, step):
        return [(self.index_at(p), self.index_at(p + step)) for p in range(self.count)]


def lead_dot(left, right, precision=None):
    return lax.dot_general(
        left, right, (((0,), (0,)), ((), ())), precision=precision, preferred_element_type=jnp.float32
    )


def exact_dot(left, right):
    return jnp.dot(left, right, precision=EXACT, preferred_element_type=jnp.float32)


def pairs_of(slots):
    found = []
    for index, (offset, core) in enumerate(slots):
        if core is None:
            found.append((offset, 1, index))
        elif core == 0:
            found.append((offset, 2, index))
    return found


def window_terms(ring, place, stored, vectors, group, steps, parts, after=()):
    rows, full = stored.shape
    new_rows = vectors.shape[0]
    taps = jnp.array(steps, jnp.int32)
    blocks_in_all = sum(len(slots) for slots in parts)
    chunk = rows // 4

    def kernel(place_ref, step_ref, stored_ref, vectors_ref, *refs):
        outs, (held, total, arrived) = refs[len(after) : -3], refs[-3:]
        i = pl.program_id(0)
        owner = lax.rem(ring.position_of(place_ref[0]) + step_ref[i] + ring.count, ring.count)
        core = place_ref[1]

        def load(index):
            rows_of = pl.ds(index * chunk, chunk)
            return pltpu.make_async_copy(stored_ref.at[rows_of], held.at[rows_of], arrived.at[index])

        @pl.when(i == 0)
        def _():
            for index in range(4):
                load(index).start()

        left = pl.ds(pl.multiple_of((2 * ring.index_at(owner) + core) * group, group), group)
        chips, base = [], 0
        for part, slots in enumerate(parts):
            for offset, blocks, first in pairs_of(slots):
                column = 2 * ring.index_at(owner + offset)
                if blocks == 1:
                    column = column + jnp.where(owner < ring.half, core, 1 - core)
                right = pl.ds(pl.multiple_of(column * group, blocks * group), blocks * group)
                here = slice((base + first) * group, (base + first + blocks) * group)
                chips.append((part, right, here, slice(first * group, (first + blocks) * group)))
            base += len(slots)
        turned_new = vectors_ref[:, left].T

        @pl.when(i == 0)
        def _():
            for _, right, here, _ in chips:
                total[:, here] = jnp.dot(turned_new, vectors_ref[:, right], preferred_element_type=jnp.float32)
            for index in range(4):
                load(index).wait()
                rows_of = slice(index * chunk, (index + 1) * chunk)
                turned = held[rows_of, left].T
                for part, right, here, there in chips:
                    added = total[:, here] + jnp.dot(turned, held[rows_of, right], preferred_element_type=jnp.float32)
                    if index < 3:
                        total[:, here] = added
                    else:
                        outs[part][0, :, there] = added.astype(jnp.bfloat16)

        if len(steps) > 1:

            @pl.when(i > 0)
            def _():
                turned = held[:, left].T
                for part, right, _, there in chips:
                    added = jnp.dot(turned, held[:, right], preferred_element_type=jnp.float32)
                    added = added + jnp.dot(turned_new, vectors_ref[:, right], preferred_element_type=jnp.float32)
                    outs[part][0, :, there] = added.astype(jnp.bfloat16)

    def out(slots):
        return pl.BlockSpec((1, group, len(slots) * group), lambda i, a, b: (i, 0, 0))

    def shape(slots):
        return jax.ShapeDtypeStruct((len(steps), group, len(slots) * group), jnp.bfloat16)

    return pl.pallas_call(
        kernel,
        grid_spec=pltpu.PrefetchScalarGridSpec(
            num_scalar_prefetch=2,
            grid=(len(steps),),
            in_specs=[MAIN, pl.BlockSpec((new_rows, full), lambda i, a, b: (0, 0))] + [ANYWHERE] * len(after),
            out_specs=[out(slots) for slots in parts],
            scratch_shapes=[
                pltpu.VMEM((rows, full), jnp.bfloat16),
                pltpu.VMEM((group, blocks_in_all * group), jnp.float32),
                pltpu.SemaphoreType.DMA((4,)),
            ],
        ),
        out_shape=[shape(slots) for slots in parts],
        compiler_params=pltpu.CompilerParams(vmem_limit_bytes=VMEM_BYTES),
        cost_estimate=LIGHT,
        name="window_terms",
    )(place, taps, stored, vectors, *after)


def add_terms(terms, index, arrived, base, count, group, after=()):
    def kernel(terms_ref, *refs):
        out_ref, own, done = refs[-3:]
        fetch = pltpu.make_async_copy(terms_ref.at[index, :, pl.ds(base * group, count * group)], own, done)
        fetch.start()
        fetch.wait()
        for k in range(count):
            cols = slice(k * group, (k + 1) * group)
            total = own[:, cols].astype(jnp.float32)
            for ref, (array, first) in zip(refs, arrived):
                place = base + k - first
                if 0 <= place < array.shape[1] // group:
                    total = total + ref[:, place * group : (place + 1) * group].astype(jnp.float32)
            out_ref[:, cols] = total.astype(jnp.bfloat16)

    return pl.pallas_call(
        kernel,
        in_specs=[MAIN] + [FAST] * len(arrived) + [ANYWHERE] * len(after),
        out_specs=FAST,
        out_shape=jax.ShapeDtypeStruct((group, count * group), jnp.bfloat16),
        scratch_shapes=[pltpu.VMEM((group, count * group), jnp.bfloat16), pltpu.SemaphoreType.DMA],
        compiler_params=pltpu.CompilerParams(vmem_limit_bytes=SMALL_BYTES),
        cost_estimate=LIGHT,
        name="add_terms",
    )(terms, *[array for array, _ in arrived], *after)


def gate(values, after):
    def kernel(*refs):
        pass

    return pl.pallas_call(
        kernel,
        in_specs=[MAIN] * len(values) + [ANYWHERE] * len(after),
        out_specs=[MAIN] * len(values),
        out_shape=[jax.ShapeDtypeStruct(value.shape, value.dtype) for value in values],
        input_output_aliases={index: index for index in range(len(values))},
        compiler_params=pltpu.CompilerParams(vmem_limit_bytes=SMALL_BYTES),
        cost_estimate=LIGHT,
        name="gate",
    )(*values, *after)


def close_window(terms, base, ahead, back, slots, group, after=()):
    count = len(slots)
    chips = [chip for chip in pairs_of(slots) if chip[0] != 0]
    index = terms.shape[0] - 1

    def kernel(terms_ref, ahead_ref, back_ref, *refs):
        blocks_ref, turned_refs, (own, done) = refs[len(after)], refs[len(after) + 1 : -2], refs[-2:]
        fetch = pltpu.make_async_copy(terms_ref.at[index], own, done)
        fetch.start()
        fetch.wait()
        for k in range(count):
            cols = slice(k * group, (k + 1) * group)
            total = own[:, (base + k) * group : (base + k + 1) * group].astype(jnp.float32)
            total = total + ahead_ref[:, cols].astype(jnp.float32) + back_ref[:, cols].astype(jnp.float32)
            total = total.astype(jnp.bfloat16)
            blocks_ref[k] = total
            for (_, blocks, first), turned_ref in zip(chips, turned_refs):
                if first <= k < first + blocks:
                    turned_ref[k - first] = total.T

    sizes = [count] + [blocks for _, blocks, _ in chips]
    return pl.pallas_call(
        kernel,
        in_specs=[MAIN, FAST, FAST] + [ANYWHERE] * len(after),
        out_specs=[FAST] * len(sizes),
        out_shape=[jax.ShapeDtypeStruct((size, group, group), jnp.bfloat16) for size in sizes],
        scratch_shapes=[pltpu.VMEM(terms.shape[1:], jnp.bfloat16), pltpu.SemaphoreType.DMA],
        compiler_params=pltpu.CompilerParams(vmem_limit_bytes=SMALL_BYTES),
        cost_estimate=LIGHT,
        name="close_window",
    )(terms, ahead, back, *after)


def rough_dot(left, right):
    return jnp.dot(left.astype(jnp.bfloat16), right.astype(jnp.bfloat16), preferred_element_type=jnp.float32)


def split_terms(value):
    high = value.astype(jnp.bfloat16)
    value = value - high.astype(jnp.float32)
    middle = value.astype(jnp.bfloat16)
    value = value - middle.astype(jnp.float32)
    return high, middle, value.astype(jnp.bfloat16)


def identity(size):
    rows = lax.broadcasted_iota(jnp.int32, (size, size), 0)
    cols = lax.broadcasted_iota(jnp.int32, (size, size), 1)
    return (rows == cols).astype(jnp.float32)


def eliminate(matrix_ref, right_ref, out_ref, work, block):
    size = matrix_ref.shape[0]
    work[...] = matrix_ref[...]
    out_ref[...] = right_ref[...]
    eye = identity(block)
    for start in range(0, size, block):
        here = slice(start, start + block)
        rest = slice(start + block, size)
        corner = work[here, here]
        norm = jnp.max(jnp.sum(jnp.abs(corner), axis=0))

        def unfinished(state):
            return jnp.logical_and(state[0] < 40, state[1] > 5e-5)

        def improve(state):
            step, _, inverse = state
            better = inverse + exact_dot(inverse, eye - exact_dot(work[here, here], inverse))
            left_over = eye - exact_dot(work[here, here], better)
            return step + 1, jnp.max(jnp.abs(left_over)), better

        found = lax.while_loop(unfinished, improve, (jnp.int32(0), jnp.float32(1.0), eye / norm))[2]
        found = found + exact_dot(found, eye - exact_dot(work[here, here], found))
        solved = exact_dot(found, out_ref[here, :])
        out_ref[here, :] = solved
        if start + block < size:
            across = exact_dot(found, work[here, rest])
            down = work[rest, here]
            work[rest, rest] = work[rest, rest] - exact_dot(down, across)
            out_ref[rest, :] = out_ref[rest, :] - exact_dot(down, solved)
            work[here, rest] = across
    for start in range(size - 2 * block, -1, -block):
        here = slice(start, start + block)
        rest = slice(start + block, size)
        out_ref[here, :] = out_ref[here, :] - exact_dot(work[here, rest], out_ref[rest, :])


def solve(place, pairs_count, mine, other, kept, came, after=()):
    group, width = mine.shape
    examples = 2 * kept.shape[0]
    size = kept.shape[0] // pairs_count

    def kernel(place_ref, mine_ref, other_ref, kept_ref, came_ref, *refs):
        out_ref, pairs_ref, matrix, right, power, inverse, first_ref = refs[len(after) :]
        for start in range(0, kept_ref.shape[0], size):
            near, far = kept_ref[start : start + size, :width], came_ref[start : start + size, :width]
            even = lax.rem(place_ref[0], 2) == 0
            first_ref[2 * start : 2 * start + size, :] = jnp.where(even, near, far)
            first_ref[2 * start + size : 2 * start + 2 * size, :] = jnp.where(even, far, near)
        eye = identity(width)
        t = place_ref[1]
        matrix[pl.ds(pl.multiple_of(t * group, group), group), :] = mine_ref[...]
        matrix[pl.ds(pl.multiple_of((1 - t) * group, group), group), :] = other_ref[...]
        turned = first_ref[...].T
        full = matrix[...] + jnp.dot(turned, first_ref[...], preferred_element_type=jnp.float32) + damping * eye
        diagonal = full * eye
        rows_scale = lax.rsqrt(jnp.sum(diagonal, axis=1, keepdims=True))
        cols_scale = lax.rsqrt(jnp.sum(diagonal, axis=0, keepdims=True))
        full = full * rows_scale * cols_scale
        matrix[...] = full
        right[...] = turned.astype(jnp.float32) * rows_scale

        sums = jnp.max(jnp.sum(jnp.abs(full), axis=0))
        squared = rough_dot(full, full)
        norm = jnp.sqrt(jnp.max(jnp.sum(jnp.abs(squared), axis=0)) + sums * sums / 128)
        start = eye - full / norm
        inverse[...] = eye + start
        power[...] = start.astype(jnp.bfloat16)
        for _ in range(7):
            raised = jnp.dot(power[...], power[...], preferred_element_type=jnp.float32).astype(jnp.bfloat16)
            power[...] = raised
            held = inverse[...]
            inverse[...] = held + jnp.dot(held.astype(jnp.bfloat16), raised, preferred_element_type=jnp.float32)
        power[...] = (inverse[...] / norm).astype(jnp.bfloat16)

        largest = jnp.max(jnp.abs(right[...]))
        out_ref[...] = jnp.dot(power[...], right[...].astype(jnp.bfloat16), preferred_element_type=jnp.float32)

        def unfinished(state):
            return jnp.logical_and(state[0] < 12, jnp.logical_not(state[1] <= 5e-5 * largest))

        def refine(state):
            left_over = right[...] - exact_dot(matrix[...], out_ref[...])
            change = jnp.dot(power[...], left_over.astype(jnp.bfloat16), preferred_element_type=jnp.float32)
            out_ref[...] = out_ref[...] + change
            return state[0] + 1, jnp.max(jnp.abs(left_over))

        worst = lax.while_loop(unfinished, refine, (jnp.int32(0), 1.0 + largest))[1]

        @pl.when(jnp.logical_not(worst <= 5e-5 * largest))
        def _():
            eliminate(matrix, right, out_ref, inverse, 128)

        solved = out_ref[...] * rows_scale
        out_ref[...] = solved
        pairs = jnp.zeros((examples, examples), jnp.float32)
        for term in split_terms(solved):
            pairs = pairs + jnp.dot(first_ref[...], term, preferred_element_type=jnp.float32)
        pairs_ref[...] = pairs

    whole = pl.BlockSpec(memory_space=pltpu.VMEM)
    return pl.pallas_call(
        kernel,
        in_specs=[pl.BlockSpec(memory_space=pltpu.SMEM)] + [whole] * 4 + [ANYWHERE] * len(after),
        out_shape=[
            jax.ShapeDtypeStruct((width, examples), jnp.float32),
            jax.ShapeDtypeStruct((examples, examples), jnp.float32),
        ],
        scratch_shapes=[
            pltpu.VMEM((width, width), jnp.float32),
            pltpu.VMEM((width, examples), jnp.float32),
            pltpu.VMEM((width, width), jnp.bfloat16),
            pltpu.VMEM((width, width), jnp.float32),
            pltpu.VMEM((examples, width), jnp.bfloat16),
        ],
        compiler_params=pltpu.CompilerParams(vmem_limit_bytes=VMEM_BYTES),
        cost_estimate=LIGHT,
        name="solve",
    )(place, mine, other, kept, came, *after)


def spread_back(place, stored, solved, owners, group, after=()):
    rows = stored.shape[0]
    width, examples = solved.shape
    pairs = owners // 2

    def kernel(place_ref, first_ref, solved_ref, *refs):
        cols, outs = refs[:owners], refs[owners + len(after) :]
        total = jnp.zeros((rows, examples), jnp.float32)
        for term in split_terms(solved_ref[...]):
            total = total + jnp.dot(first_ref[...], term, preferred_element_type=jnp.float32)
        terms = jnp.concatenate(split_terms(total.T)[:2], axis=0)
        for index in range(owners):
            product = jnp.dot(terms, cols[index][...], preferred_element_type=jnp.float32)
            outs[index // 2][index % 2] = (product[:examples] + product[examples:]).astype(jnp.bfloat16)

    def owner(index, ref):
        return 2 * lax.rem(ref[0] // 2 + index // 2, pairs) + index % 2

    return pl.pallas_call(
        kernel,
        grid_spec=pltpu.PrefetchScalarGridSpec(
            num_scalar_prefetch=1,
            grid=(1,),
            in_specs=[
                pl.BlockSpec((rows, width), lambda i, ref: (0, 0)),
                pl.BlockSpec((width, examples), lambda i, ref: (0, 0)),
            ]
            + [
                pl.BlockSpec((rows, group), lambda i, ref, index=index: (0, 2 * owner(index, ref) + ref[1]))
                for index in range(owners)
            ]
            + [ANYWHERE] * len(after),
            out_specs=[pl.BlockSpec((2, examples, group), lambda i, ref: (0, 0, 0))] * pairs,
        ),
        out_shape=[jax.ShapeDtypeStruct((2, examples, group), jnp.bfloat16)] * pairs,
        compiler_params=pltpu.CompilerParams(vmem_limit_bytes=VMEM_BYTES),
        cost_estimate=LIGHT,
        name="spread_back",
    )(place, stored, solved, *([stored] * owners), *after)


def sum_pieces(place, came, after=()):
    _, examples, group = came[0].shape

    def kernel(place_ref, *refs):
        mine_ref, away_ref = refs[-2:]
        side = lax.rem(place_ref[0], 2)
        totals = [sum(ref[half].astype(jnp.float32) for ref in refs[: len(came)]) for half in (0, 1)]
        mine_ref[...] = jnp.where(side == 0, totals[0], totals[1])
        away_ref[...] = jnp.where(side == 0, totals[1], totals[0]).astype(jnp.bfloat16)

    return pl.pallas_call(
        kernel,
        in_specs=[pl.BlockSpec(memory_space=pltpu.SMEM)] + [FAST] * len(came) + [ANYWHERE] * len(after),
        out_specs=[FAST, FAST],
        out_shape=[
            jax.ShapeDtypeStruct((examples, group), jnp.float32),
            jax.ShapeDtypeStruct((examples, group), jnp.bfloat16),
        ],
        compiler_params=pltpu.CompilerParams(vmem_limit_bytes=SMALL_BYTES),
        cost_estimate=LIGHT,
        name="sum_pieces",
    )(place, *came, *after)


def pair_products(place, own_cols, first_pairs, mine, other, solved, after=()):
    examples, group = own_cols.shape

    def kernel(place_ref, own_ref, first_ref, mine_ref, other_ref, solved_ref, *refs):
        g = 2 * place_ref[0] + place_ref[1]
        own = own_ref[...]
        damped = solved_ref[pl.ds(pl.multiple_of(place_ref[1] * group, group), group), :].T
        rest = own - lax.dot_general(
            first_ref[...], own, (((0,), (0,)), ((), ())), precision=EXACT, preferred_element_type=jnp.float32
        )
        rest = rest - mine_ref[...] - other_ref[...].astype(jnp.float32) - jnp.where(g < 2, damping * damped, 0.0)
        products = lax.dot_general(
            rest, rest, (((1,), (1,)), ((), ())), precision=EXACT, preferred_element_type=jnp.float32
        )
        refs[-1][...] = products + jnp.where(g == 0, first_ref[...], 0.0)

    return pl.pallas_call(
        kernel,
        in_specs=[pl.BlockSpec(memory_space=pltpu.SMEM)] + [FAST] * 5 + [ANYWHERE] * len(after),
        out_specs=FAST,
        out_shape=jax.ShapeDtypeStruct((examples, examples), jnp.float32),
        compiler_params=pltpu.CompilerParams(vmem_limit_bytes=SMALL_BYTES),
        cost_estimate=LIGHT,
        name="pair_products",
    )(place, own_cols, first_pairs, mine, other, solved, *after)


def assembly_tables(ring, slots, d, t):
    start = [0] * ring.count
    arrived = [0] * ring.count
    for offset, _, first in pairs_of(slots):
        start[offset % ring.count] = first
    place = len(slots)
    for offset in ring.offsets:
        start[-offset % ring.count] = place
        arrived[-offset % ring.count] = 1
        place += 2
    here = ring.position_of(d)
    early = here < ring.half

    def look_up(values, offset):
        found = jnp.zeros_like(offset)
        for index, value in enumerate(values):
            if value:
                found = jnp.where(offset == index, value, found)
        return found

    def offsets_of(chips):
        return lax.rem(ring.position_of(chips) - here + 2 * ring.count, ring.count)

    def fetch(offset, j):
        own = (j == t) == early
        quarter = jnp.where(own, start[ring.half], place)
        return jnp.where(offset == ring.half, quarter, look_up(start, offset) + j)

    chips = jnp.arange(ring.half, dtype=jnp.int32)
    j = jnp.arange(2, dtype=jnp.int32)[None, :]
    send = fetch(offsets_of((1 - t) * ring.half + chips)[:, None], j)
    offset = offsets_of(t * ring.half + chips)[:, None, None]
    r = jnp.arange(2, dtype=jnp.int32)[None, :, None]
    u = jnp.arange(2, dtype=jnp.int32)[None, None, :]
    by_columns = jnp.where(offset == ring.half, early.astype(jnp.int32), look_up(arrived, offset)) == 1
    j = jnp.where(by_columns, r, u)
    local = fetch(offset, j)
    other = 2 * chips[:, None, None] + j
    mine = (jnp.where(by_columns, u, r) == t).astype(jnp.int32)
    final = jnp.stack([local, other, mine]).reshape(-1)
    return send.reshape(-1).astype(jnp.int32), final.astype(jnp.int32)


def for_sibling(table, blocks, group):
    total = table.shape[0]
    wide = min(4, total)

    def kernel(table_ref, *refs):
        for k in range(wide):
            refs[-1][k] = refs[k][0]

    return pl.pallas_call(
        kernel,
        grid_spec=pltpu.PrefetchScalarGridSpec(
            num_scalar_prefetch=1,
            grid=(total // wide,),
            in_specs=[
                pl.BlockSpec((1, group, group), lambda c, ref, k=k: (ref[wide * c + k], 0, 0)) for k in range(wide)
            ],
            out_specs=pl.BlockSpec((wide, group, group), lambda c, ref: (c, 0, 0)),
        ),
        out_shape=jax.ShapeDtypeStruct((total, group, group), jnp.bfloat16),
        compiler_params=pltpu.CompilerParams(vmem_limit_bytes=SMALL_BYTES),
        cost_estimate=LIGHT,
        name="for_sibling",
    )(table, *([blocks] * wide))


def finish(place, table, blocks, other, half, group):
    wide = half // 2
    total = 4 * half

    def at(kind, r, c, k, u, ref):
        return ref[kind * total + 4 * (wide * c + k) + 2 * r + u]

    def spec(kind, k, u):
        return pl.BlockSpec((1, group, group), lambda r, c, ref, place: (at(kind, r, c, k, u, ref), 0, 0))

    order = [(k, u) for k in range(wide) for u in (0, 1)]

    def kernel(table_ref, place_ref, *refs):
        r, c = pl.program_id(0), pl.program_id(1)
        out_ref = refs[-1]
        shape = (group, group)
        gap = lax.broadcasted_iota(jnp.int32, shape, 1) - lax.broadcasted_iota(jnp.int32, shape, 0)
        for index, (k, u) in enumerate(order):
            cols = slice(index * group, (index + 1) * group)
            chip = place_ref[1] * half + wide * c + k
            apart = (2 * place_ref[0] + r - 2 * chip - u) * group
            added = jnp.where(gap == apart, jnp.float32(damping), jnp.float32(0.0))
            mine = at(2, r, c, k, u, table_ref) == 1

            @pl.when(mine)
            def _():
                out_ref[:, cols] = added + refs[index][0].astype(jnp.float32)

            @pl.when(jnp.logical_not(mine))
            def _():
                out_ref[:, cols] = added + refs[len(order) + index][0].astype(jnp.float32)

    return pl.pallas_call(
        kernel,
        grid_spec=pltpu.PrefetchScalarGridSpec(
            num_scalar_prefetch=2,
            grid=(2, 2),
            in_specs=[spec(0, k, u) for k, u in order] + [spec(1, k, u) for k, u in order],
            out_specs=pl.BlockSpec((group, 2 * wide * group), lambda r, c, ref, place: (r, c)),
        ),
        out_shape=jax.ShapeDtypeStruct((2 * group, 2 * half * group), jnp.float32),
        compiler_params=pltpu.CompilerParams(vmem_limit_bytes=SMALL_BYTES),
        cost_estimate=LIGHT,
        name="finish",
    )(table, place, *([blocks] * len(order)), *([other] * len(order)))


def in_order(index, mine, other, axis):
    return jnp.where(
        index == 0,
        jnp.concatenate([mine, other], axis=axis),
        jnp.concatenate([other, mine], axis=axis),
    )


def pair_swap(value, count):
    return lax.ppermute(value, "dp", [(index, index ^ 1) for index in range(count)])


def far_shift(value, step, count):
    return lax.ppermute(value, "dp", [(index, (index + 2 * step) % count) for index in range(count)])


def exchange_pairs(slice_of, pair, count):
    pairs = count // 2
    came = [slice_of(pair)]
    for step in range(1, pairs):
        came.append(far_shift(slice_of(lax.rem(pair + step, pairs)), step, count))
    return came


def natural(came, pair):
    pairs = len(came)
    pieces = []
    for index in range(pairs):
        behind = lax.rem(pair - index + pairs, pairs)
        piece = came[0]
        for step in range(1, pairs):
            piece = jnp.where(behind == step, came[step], piece)
        pieces.append(piece)
    return pieces


def scatter_pairs(value, pair, count):
    size = value.shape[0] // (count // 2)

    def slice_of(index):
        return lax.dynamic_slice_in_dim(value, index * size, size, 0)

    return sum(piece.astype(jnp.float32) for piece in exchange_pairs(slice_of, pair, count))


def local(ring, activations, out_grads, proj_in, proj_out, stored, counts, query_ids):
    owners = ring.count
    full = stored.shape[1]
    width = full // owners
    group = width // 2
    half = ring.half
    t = lax.axis_index("tensor")
    d = lax.axis_index("dp")
    pair, side = d // 2, lax.rem(d, 2)
    g = 2 * d + t
    place = jnp.stack([d, t]).astype(jnp.int32)

    pairs_count = owners // 2
    first_stored = stored[:, :width]
    corner_rows = lead_dot(lax.dynamic_slice_in_dim(first_stored, t * group, group, 1), first_stored)
    corner_payload = scatter_pairs(corner_rows, pair, owners)

    sides = jnp.concatenate(
        [
            jnp.dot(activations, proj_in, preferred_element_type=jnp.float32),
            jnp.dot(out_grads, proj_out, preferred_element_type=jnp.float32),
        ],
        axis=1,
    )
    sides = sides + lax.ppermute(sides, "tensor", SWAP)

    examples = counts.shape[0]
    all_examples = examples * owners
    rank = proj_in.shape[1]
    position = jnp.arange(SEQ, dtype=jnp.int32)[None, :]
    weights = jnp.where(
        position < counts[:, None], 1.0 / counts.astype(jnp.float32)[:, None], jnp.float32(0.0)
    )
    outer = jnp.einsum(
        "es,esi,esj->eij",
        weights,
        sides[:, :rank].reshape(examples, SEQ, rank),
        sides[:, rank:].reshape(examples, SEQ, rank),
        precision=EXACT,
    )
    vectors = outer.reshape(examples, full).astype(jnp.bfloat16)

    def columns_for(index):
        groups = [lax.dynamic_slice_in_dim(vectors, (4 * index + 2 * s + t) * group, group, 1) for s in (0, 1)]
        return jnp.concatenate([vectors[:, :width]] + groups, axis=1)

    payloads = [columns_for(lax.rem(pair + step, pairs_count)) for step in range(pairs_count)]

    split = (len(ring.offsets) + 1) // 2
    far_slots = [(half, None)]
    for offset in ring.offsets[:split]:
        far_slots += [(offset, 0), (offset, 1)]
    near_slots = []
    for offset in ring.offsets[split:] + [0]:
        near_slots += [(offset, 0), (offset, 1)]

    slots = far_slots + near_slots
    far_count, near_count = len(far_slots), len(near_slots)
    ahead, back = ring.shift(1), ring.shift(-1)

    def terms_of(steps, parts, after=()):
        return window_terms(ring, place, stored, vectors, group, steps, parts, after)

    came = [payloads[0]] + [far_shift(payloads[step], step, owners) for step in range(1, pairs_count)]
    came = jnp.concatenate(natural(came, pair), axis=0)
    second_group = jnp.concatenate([came[:, :width], came[:, width + group :]], axis=1)
    first_group = came[:, : width + group]
    kept = jnp.where(side == 0, first_group, second_group)
    away = jnp.where(side == 0, second_group, first_group)
    received = pair_swap(away, owners)
    corner_second = corner_payload + pair_swap(corner_payload, owners)
    corner_rows = [corner_second] + [far_shift(corner_second, step, owners) for step in range(1, pairs_count)]
    corner_rows = jnp.concatenate(natural(corner_rows, pair), axis=0)
    corner_other = lax.ppermute(corner_rows, "tensor", SWAP)
    far, near = terms_of([half], [far_slots, near_slots], [away, corner_second])
    far, near = far[0], near[0]
    second_steps = [half - 1, 1 - half, half - 2, 2 - half]
    far, near = gate([far, near], [corner_rows, received])
    second = terms_of(second_steps, [slots], [far])[0]
    shape = (pairs_count, 1, examples, group)
    own_cols = in_order(side, kept[:, width:].reshape(shape), received[:, width:].reshape(shape), 1)
    own_cols = own_cols.reshape(all_examples, group).astype(jnp.float32)
    far_ahead = lax.ppermute(far, "dp", ahead)
    near_back = lax.ppermute(near, "dp", back)
    total = far_count + near_count
    going = add_terms(second, 0, [(far_ahead, 0)], 0, total, group)
    coming = add_terms(second, 1, [(near_back, far_count)], 0, total, group)

    solved, first_pairs = solve(place, pairs_count, corner_rows, corner_other, kept, received, [going, coming])
    pieces = spread_back(place, stored, solved, owners, group)
    later_steps = [s for step in range(half - 3, 0, -1) for s in (step, -step)] + [0]
    for step in range(half - 2, 0, -1):
        came_ahead = lax.ppermute(going, "dp", ahead)
        came_back = lax.ppermute(coming, "dp", back)
        own, index, token = (second, 2, [pieces[0]]) if step == half - 2 else (later, later_steps.index(step), [])
        if step == 1:
            far_going = add_terms(own, index, [(came_ahead, 0)], 0, far_count, group, token)
            far_coming = add_terms(own, index + 1, [(came_back, 0)], 0, far_count, group, token)
            token = [far_going, far_coming]
            near_going = add_terms(own, index, [(came_ahead, 0)], far_count, near_count, group, token)
            near_coming = add_terms(own, index + 1, [(came_back, 0)], far_count, near_count, group, token)
            token = [near_going, near_coming]
        else:
            going = add_terms(own, index, [(came_ahead, 0)], 0, total, group, token)
            coming = add_terms(own, index + 1, [(came_back, 0)], 0, total, group, token)
            token = [going, coming]
        if step == half - 2:
            came = [pieces[0]] + [far_shift(pieces[index], index, owners) for index in range(1, pairs_count)]
            terms, away = sum_pieces(place, came)
            terms_other = pair_swap(away, owners)
            going, coming = gate([going, coming], [away])
            later = terms_of(later_steps, [slots], [going])[0]
    far_sums = [lax.ppermute(far_going, "dp", ahead), lax.ppermute(far_coming, "dp", back)]
    near_sums = [lax.ppermute(near_going, "dp", ahead), lax.ppermute(near_coming, "dp", back)]

    far = close_window(later, 0, *far_sums, far_slots, group)
    near = close_window(later, far_count, *near_sums, near_slots, group, [far[0]])
    turned = {}
    for (found, slots) in ((far, far_slots), (near, near_slots)):
        chips = [chip for chip in pairs_of(slots) if chip[0] != 0]
        for (offset, _, _), block in zip(chips, found[1:]):
            turned[offset] = block
    shifted = {
        offset: lax.ppermute(turned[offset], "dp", ring.shift(offset))
        for offset in [half] + ring.offsets
    }
    came = [shifted[offset] for offset in ring.offsets + [half]]
    early = [shifted[offset] for offset in [half] + ring.offsets[:split]]
    pairs = pair_products(place, own_cols, first_pairs, terms, terms_other, solved, early)
    bit = owners // 2
    while bit >= 1:
        kept_rows = jnp.where((d & bit) == 0, pairs[: pairs.shape[0] // 2], pairs[pairs.shape[0] // 2 :])
        sent_rows = jnp.where((d & bit) == 0, pairs[pairs.shape[0] // 2 :], pairs[: pairs.shape[0] // 2])
        pairs = kept_rows + lax.ppermute(sent_rows, "dp", [(index, index ^ bit) for index in range(owners)])
        bit //= 2
    pairs = pairs + lax.ppermute(pairs, "tensor", SWAP)
    chosen = (query_ids[:, None] == jnp.arange(all_examples, dtype=jnp.int32)[None, :]).astype(jnp.float32)
    scores = lax.dot_general(chosen, pairs, (((1,), (1,)), ((), ())), precision=EXACT, preferred_element_type=jnp.float32) / R
    blocks = jnp.concatenate([far[0], near[0]] + came, axis=0)
    send_table, final_table = assembly_tables(ring, far_slots + near_slots, d, t)
    other = lax.ppermute(for_sibling(send_table, blocks, group), "tensor", SWAP)
    return finish(place, final_table, blocks, other, half, group), scores


def solution(mesh):
    placed = (
        P(("groups", "dp"), "tensor"),
        P(("groups", "dp"), "tensor"),
        P("tensor", None),
        P("tensor", None),
        P(("groups", "dp"), None),
        P(("groups", "dp")),
        P("groups"),
    )
    ring = Ring(mesh)

    def program(*args):
        return local(ring, *args)

    return jax.shard_map(
        program,
        mesh=mesh,
        in_specs=placed,
        out_specs=(P(("groups", "dp"), "tensor"), P("groups", "dp")),
        check_vma=False,
    )
```

profile of v0, /device:TPU:0, one launch (start us, length us, event | category | flops | bytes accessed | tf_op | source)
XLA Modules:
  0.0 231.0 jit_solution(3685768184703643035)
XLA Ops:
  0.7 6.1 %fusion.29 = f32[256,64]{0,1:T(8,128)S(1)} fusion(bf16[256,14336]{1,0:T(8,128)(2,1)} %param.10, bf16[14336,64]{0,1:T(8,128)(2,1)} %param.12), kind=kOutput, calls=%fused_computation.118 | convolution fusion | flops 469762048 | bytes 9240576 | tf_op jit(solution)/shard_map/dot_general | solution.py:649
  10.0 2.9 %collective-permute-start.4 = (f32[64,512]{1,0:T(8,128)}, f32[64,512]{1,0:T(8,128)S(1)}, u32[]{:S(2)}, u32[]{:S(2)}) collective-permute-start(f32[64,512]{1,0:T(8,128)} %get-tuple-element.48), channel_id=1, source_target_pairs={{0,4},{2,6},{4,8},{6,10},{8,12},{10,14},{12,0},{14,2},{1,5},{3,7},... | collective-permute-start | bytes 393224 | tf_op jit(solution)/shard_map/ppermute | solution.py:598
  13.0 2.0 collective-permute-start.6
  18.5 1.6 collective-permute-start.3
  20.5 3.6 %collective-permute-start.1 = (bf16[16,1024]{1,0:T(8,128)(2,1)S(1)}, bf16[16,1024]{1,0:T(8,128)(2,1)S(1)}, u32[]{:S(2)}, u32[]{:S(2)}) collective-permute-start(bf16[16,1024]{1,0:T(8,128)(2,1)S(1)} %get-tuple-element.67), channel_id=1, source_target_pairs={{0,12},{2,14},{4,0},{6,2},{8,4},{10,6},{12,8},{14,10},{1,13},{3,15... | collective-permute-start | bytes 98312 | tf_op jit(solution)/shard_map/ppermute | solution.py:598
  24.2 4.9 %collective-permute-done.5 = f32[64,512]{1,0:T(8,128)} collective-permute-done((f32[64,512]{1,0:T(8,128)S(1)}, f32[64,512]{1,0:T(8,128)}, u32[]{:S(2)}, u32[]{:S(2)}) %collective-permute-start.5) | collective-permute-done | bytes 131104 | tf_op jit(solution)/shard_map/ppermute | solution.py:598
  32.5 3.0 %collective-permute-done.7 = f32[64,512]{1,0:T(8,128)S(1)} collective-permute-done((f32[64,512]{1,0:T(8,128)S(1)}, f32[64,512]{1,0:T(8,128)S(1)}, u32[]{:S(2)}, u32[]{:S(2)}) %collective-permute-start.7) | collective-permute-done | bytes 131104 | tf_op jit(solution)/shard_map/ppermute | solution.py:594
  35.6 2.4 %collective-permute-start.9 = (f32[64,512]{1,0:T(8,128)S(1)}, f32[64,512]{1,0:T(8,128)S(1)}, u32[]{:S(2)}, u32[]{:S(2)}) collective-permute-start(f32[64,512]{1,0:T(8,128)S(1)} %add.290.refs_1_), channel_id=1, source_target_pairs={{0,8},{2,10},{4,12},{6,14},{8,0},{10,2},{12,4},{14,6},{1,9},{3,11}... | collective-permute-start | bytes 393224 | tf_op jit(solution)/shard_map/ppermute | solution.py:598
  39.4 1.6 collective-permute-start.11
  41.0 6.6 %window_terms.3 = (bf16[1,256,1280]{2,1,0:T(8,128)(2,1)}, bf16[1,256,1024]{2,1,0:T(8,128)(2,1)}) custom-call(s32[2]{0:T(128)} %pad_add_fusion.1.place_ref, s32[1]{0:T(128)} %constant.135.clone.step_ref, bf16[1024,4096]{1,0:T(8,128)(2,1)} %stored_ref.5, bf16[16,4096]{1,0:T(8,128)(2,1)} %copy-done.21, bf16[64,768]{1,0:T(8,128)(2,1)} %copy-done.26, ...), custom_call_target="tpu_custom_call" | custom-call | flops 1000000 | bytes 100000 | tf_op jit(solution)/shard_map/window_terms/pallas_call | solution.py:144
  48.9 2.2 collective-permute-start.12
  51.1 12.6 %window_terms.4.terms_ref = bf16[4,256,2304]{2,1,0:T(8,128)(2,1)} custom-call(s32[2]{0:T(128)} %pad_add_fusion.1.place_ref, s32[4]{0:T(128)} %constant.136.clone.step_ref, bf16[1024,4096]{1,0:T(8,128)(2,1)} %stored_ref.5, bf16[16,4096]{1,0:T(8,128)(2,1)} %copy-done.21, bf16[256,1280]{1,0:T(8,128)(2,1)} %copy-done.11), custom_call_target="tpu_custom_call" | custom-call | flops 1000000 | bytes 100000 | tf_op jit(solution)/shard_map/window_terms/pallas_call | solution.py:144
  63.8 2.3 %copy-done.6 = bf16[4,256,2304]{2,1,0:T(8,128)(2,1)S(1)} copy-done((bf16[4,256,2304]{2,1,0:T(8,128)(2,1)S(1)}, bf16[4,256,2304]{2,1,0:T(8,128)(2,1)}, u32[]{:S(2)}) %copy-start.6) | copy-done | bytes 4718616
  67.7 1.6 collective-permute-start.16
  70.4 1.9 collective-permute-done.14.other_ref
  73.1 21.5 %solve.1 = (f32[512,128]{1,0:T(8,128)}, f32[128,128]{1,0:T(8,128)}) custom-call(s32[2]{0:T(128)} %pad_add_fusion.1.place_ref, f32[256,512]{1,0:T(8,128)} %copy-done.9, f32[256,512]{1,0:T(8,128)} %copy-done.25, bf16[64,768]{1,0:T(8,128)(2,1)} %get-tuple-element.42.kept_ref, bf16[64,768]{1,0:T(8,128)(2,1)} %copy-done.14, bf16[256,2304]{1,0:T(8,128)(2,1)} %copy-done.8, ...), custom_call_target="tpu_custom_call" | custom-call | flops 1000000 | bytes 100000 | tf_op jit(solution)/shard_map/solve/pallas_call | solution.py:358
  94.6 8.1 %spread_back.1 = (bf16[2,128,256]{2,1,0:T(8,128)(2,1)}, bf16[2,128,256]{2,1,0:T(8,128)(2,1)}, bf16[2,128,256]{2,1,0:T(8,128)(2,1)}, bf16[2,128,256]{2,1,0:T(8,128)(2,1)}) custom-call(s32[2]{0:T(128)} %pad_add_fusion.1.place_ref, bf16[1024,4096]{1,0:T(8,128)(2,1)} %stored_ref.5, f32[512,128]{1,0:T(8,128)} %get-tuple-element.26.solved_ref, ...), custom_call_target="tpu_custom_call" | custom-call | flops 1000000 | bytes 100000 | tf_op jit(solution)/shard_map/spread_back/pallas_call | solution.py:396
  102.7 2.0 collective-permute-start.17
  104.7 2.7 %collective-permute-start.19 = (bf16[2,128,256]{2,1,0:T(8,128)(2,1)}, bf16[2,128,256]{2,1,0:T(8,128)(2,1)S(1)}, u32[]{:S(2)}, u32[]{:S(2)}) collective-permute-start(bf16[2,128,256]{2,1,0:T(8,128)(2,1)} %get-tuple-element.30), channel_id=1, source_target_pairs={{0,12},{2,14},{4,0},{6,2},{8,4},{10,6},{12,8},{14,10},{1,13},{3,15... | collective-permute-start | bytes 393224 | tf_op jit(solution)/shard_map/ppermute | solution.py:598
  107.4 3.8 %collective-permute-done.17.refs_1_ = bf16[2,128,256]{2,1,0:T(8,128)(2,1)S(1)} collective-permute-done((bf16[2,128,256]{2,1,0:T(8,128)(2,1)}, bf16[2,128,256]{2,1,0:T(8,128)(2,1)S(1)}, u32[]{:S(2)}, u32[]{:S(2)}) %collective-permute-start.17) | collective-permute-done | bytes 131104 | tf_op jit(solution)/shard_map/ppermute | solution.py:598
  111.2 4.8 %collective-permute-done.18.refs_2_ = bf16[2,128,256]{2,1,0:T(8,128)(2,1)S(1)} collective-permute-done((bf16[2,128,256]{2,1,0:T(8,128)(2,1)}, bf16[2,128,256]{2,1,0:T(8,128)(2,1)S(1)}, u32[]{:S(2)}, u32[]{:S(2)}) %collective-permute-start.18) | collective-permute-done | bytes 131104 | tf_op jit(solution)/shard_map/ppermute | solution.py:598
  117.6 2.8 %add_terms.11.refs_1_ = bf16[256,2304]{1,0:T(8,128)(2,1)} custom-call(bf16[4,256,2304]{2,1,0:T(8,128)(2,1)S(1)} %bitcast.24, bf16[256,2304]{1,0:T(8,128)(2,1)} %collective-permute-done.16.refs_0_, bf16[2,128,256]{2,1,0:T(8,128)(2,1)S(1)} %copy-done.12), custom_call_target="tpu_custom_call" | custom-call | flops 1000000 | bytes 100000 | tf_op jit(solution)/shard_map/add_terms/pallas_call | solution.py:179
  120.5 1.8 add_terms.10.refs_0_
  122.3 3.3 %collective-permute-start.20 = (bf16[256,2304]{1,0:T(8,128)(2,1)S(1)}, bf16[256,2304]{1,0:T(8,128)(2,1)}, u32[]{:S(2)}, u32[]{:S(2)}) collective-permute-start(bf16[256,2304]{1,0:T(8,128)(2,1)S(1)} %get-tuple-element.32.refs_0_), channel_id=1, source_target_pairs={{0,4},{4,8},{8,12},{12,14},{14,10},{10,6},{6,2},{2,0},{1,5},{5,9},... | collective-permute-start | bytes 3538952 | tf_op jit(solution)/shard_map/ppermute | solution.py:722
  125.7 10.6 %window_terms.5.terms_ref = bf16[3,256,2304]{2,1,0:T(8,128)(2,1)} custom-call(s32[2]{0:T(128)} %pad_add_fusion.1.place_ref, s32[3]{0:T(128)} %constant.137.clone.step_ref, bf16[1024,4096]{1,0:T(8,128)(2,1)} %stored_ref.5, bf16[16,4096]{1,0:T(8,128)(2,1)} %copy-done.21, bf16[256,2304]{1,0:T(8,128)(2,1)} %copy-done.7), custom_call_target="tpu_custom_call" | custom-call | flops 1000000 | bytes 100000 | tf_op jit(solution)/shard_map/window_terms/pallas_call | solution.py:144
  136.3 14.7 %collective-permute-done.20.refs_0_ = bf16[256,2304]{1,0:T(8,128)(2,1)} collective-permute-done((bf16[256,2304]{1,0:T(8,128)(2,1)S(1)}, bf16[256,2304]{1,0:T(8,128)(2,1)}, u32[]{:S(2)}, u32[]{:S(2)}) %collective-permute-start.20) | collective-permute-done | bytes 1179680 | tf_op jit(solution)/shard_map/ppermute | solution.py:722
  151.0 2.0 copy-done.1
  154.5 2.6 %collective-permute-start.21 = (bf16[256,1280]{1,0:T(8,128)(2,1)S(1)}, bf16[256,1280]{1,0:T(8,128)(2,1)}, u32[]{:S(2)}, u32[]{:S(2)}) collective-permute-start(bf16[256,1280]{1,0:T(8,128)(2,1)S(1)} %add_terms.12.refs_1_), channel_id=1, source_target_pairs={{0,4},{4,8},{8,12},{12,14},{14,10},{10,6},{6,2},{2,0},{1,5},{5,9},... | collective-permute-start | bytes 1966088 | tf_op jit(solution)/shard_map/ppermute | solution.py:742
  158.8 2.2 add_terms.14
  161.1 2.1 collective-permute-start.24
  163.1 2.2 add_terms.15
  166.4 6.3 %collective-permute-done.21.ahead_ref = bf16[256,1280]{1,0:T(8,128)(2,1)} collective-permute-done((bf16[256,1280]{1,0:T(8,128)(2,1)S(1)}, bf16[256,1280]{1,0:T(8,128)(2,1)}, u32[]{:S(2)}, u32[]{:S(2)}) %collective-permute-start.21) | collective-permute-done | bytes 655392 | tf_op jit(solution)/shard_map/ppermute | solution.py:742
  172.7 3.8 %collective-permute-done.23.back_ref = bf16[256,1280]{1,0:T(8,128)(2,1)} collective-permute-done((bf16[256,1280]{1,0:T(8,128)(2,1)S(1)}, bf16[256,1280]{1,0:T(8,128)(2,1)}, u32[]{:S(2)}, u32[]{:S(2)}) %collective-permute-start.23) | collective-permute-done | bytes 655392 | tf_op jit(solution)/shard_map/ppermute | solution.py:742
  176.5 2.0 copy-done.2
  178.5 2.0 close_window.2
  182.3 3.7 %collective-permute-start.29 = (bf16[1,256,256]{2,1,0:T(8,128)(2,1)S(1)}, bf16[1,256,256]{2,1,0:T(8,128)(2,1)S(1)}, u32[]{:S(2)}, u32[]{:S(2)}) collective-permute-start(bf16[1,256,256]{2,1,0:T(8,128)(2,1)S(1)} %get-tuple-element.39), channel_id=1, source_target_pairs={{0,14},{4,10},{8,6},{12,2},{14,0},{10,4},{6,8},{2,12},{1,15},{5,11... | collective-permute-start | bytes 393224 | tf_op jit(solution)/shard_map/ppermute | solution.py:753
  186.1 4.1 %collective-permute-start.31 = (bf16[128,256]{1,0:T(8,128)(2,1)S(1)}, bf16[128,256]{1,0:T(8,128)(2,1)S(1)}, u32[]{:S(2)}, u32[]{:S(2)}) collective-permute-start(bf16[128,256]{1,0:T(8,128)(2,1)S(1)} %get-tuple-element.31.refs_2_), channel_id=1, source_target_pairs={{0,2},{2,0},{4,6},{6,4},{8,10},{10,8},{12,14},{14,12},{1,3},{3,1},... | collective-permute-start | bytes 196616 | tf_op jit(solution)/shard_map/ppermute | solution.py:594
  190.2 1.7 close_window.3
  192.1 3.2 %collective-permute-done.31.other_ref = bf16[128,256]{1,0:T(8,128)(2,1)S(1)} collective-permute-done((bf16[128,256]{1,0:T(8,128)(2,1)S(1)}, bf16[128,256]{1,0:T(8,128)(2,1)S(1)}, u32[]{:S(2)}, u32[]{:S(2)}) %collective-permute-start.31) | collective-permute-done | bytes 65568 | tf_op jit(solution)/shard_map/ppermute | solution.py:594
  195.3 4.3 %collective-permute-done.29.refs_0_ = bf16[1,256,256]{2,1,0:T(8,128)(2,1)S(1)} collective-permute-done((bf16[1,256,256]{2,1,0:T(8,128)(2,1)S(1)}, bf16[1,256,256]{2,1,0:T(8,128)(2,1)S(1)}, u32[]{:S(2)}, u32[]{:S(2)}) %collective-permute-start.29) | collective-permute-done | bytes 131104 | tf_op jit(solution)/shard_map/ppermute | solution.py:753
  200.1 7.3 %collective-permute-done.27.refs_2_ = bf16[2,256,256]{2,1,0:T(8,128)(2,1)S(1)} collective-permute-done((bf16[2,256,256]{2,1,0:T(8,128)(2,1)S(1)}, bf16[2,256,256]{2,1,0:T(8,128)(2,1)S(1)}, u32[]{:S(2)}, u32[]{:S(2)}) %collective-permute-start.27) | collective-permute-done | bytes 262176 | tf_op jit(solution)/shard_map/ppermute | solution.py:753
  208.6 6.0 %collective-permute-start.32 = (f32[64,128]{1,0:T(8,128)S(1)}, f32[64,128]{1,0:T(8,128)S(1)}, u32[]{:S(2)}, u32[]{:S(2)}) collective-permute-start(f32[64,128]{1,0:T(8,128)S(1)} %slice_select_fusion), channel_id=1, source_target_pairs={{0,8},{2,10},{4,12},{6,14},{8,0},{10,2},{12,4},{14,6},{1,9},{3,11}... | collective-permute-start | bytes 98312 | tf_op jit(solution)/shard_map/ppermute | solution.py:763
  214.7 1.8 collective-permute-done.32
  216.6 1.6 for_sibling.1
  218.3 2.0 collective-permute-done.33
  220.7 3.4 %collective-permute-done.34 = f32[16,128]{1,0:T(8,128)S(1)} collective-permute-done((f32[16,128]{1,0:T(8,128)S(1)}, f32[16,128]{1,0:T(8,128)S(1)}, u32[]{:S(2)}, u32[]{:S(2)}) %collective-permute-start.34) | collective-permute-done | bytes 8224 | tf_op jit(solution)/shard_map/ppermute | solution.py:763
  226.1 1.6 copy-done.5
  227.7 3.3 %finish.1 = f32[512,2048]{1,0:T(8,128)} custom-call(s32[48]{0:T(128)S(1)} %reshape.231.table_ref, s32[2]{0:T(128)S(1)} %copy-done.20, bf16[16,256,256]{2,1,0:T(8,128)(2,1)S(1)} %copy-done.5, bf16[16,256,256]{2,1,0:T(8,128)(2,1)S(1)} %copy-done.5, bf16[16,256,256]{2,1,0:T(8,128)(2,1)S(1)} %copy-done.5, bf16[16,256,256]{2,1,0:T(8,128)(2,1)S(1)} %copy-done.5, ...), custom_call_target="tpu_custom_call" | custom-call | flops 1000000 | bytes 100000 | tf_op jit(solution)/shard_map/finish/pallas_call | solution.py:570
  (166 shorter events, 28.7 us)
Async XLA Ops:
  7.5 9.2 %collective-permute-start = (f32[256,128]{0,1:T(8,128)S(1)}, f32[256,128]{0,1:T(8,128)S(1)}, u32[]{:S(2)}, u32[]{:S(2)}) collective-permute-start(f32[256,128]{0,1:T(8,128)S(1)} %pad_maximum_fusion.1), channel_id=1, source_target_pairs={{0,1},{1,0},{2,3},{3,2},{4,5},{5,4},{6,7},{7,6},{8,9},{9,8},{10,11... | collective-permute-start | bytes 393224 | tf_op jit(solution)/shard_map/ppermute | solution.py:654
  10.0 10.5 %collective-permute-start.4 = (f32[64,512]{1,0:T(8,128)}, f32[64,512]{1,0:T(8,128)S(1)}, u32[]{:S(2)}, u32[]{:S(2)}) collective-permute-start(f32[64,512]{1,0:T(8,128)} %get-tuple-element.48), channel_id=1, source_target_pairs={{0,4},{2,6},{4,8},{6,10},{8,12},{10,14},{12,0},{14,2},{1,5},{3,7},... | collective-permute-start | bytes 393224 | tf_op jit(solution)/shard_map/ppermute | solution.py:598
  13.0 11.2 %collective-permute-start.6 = (f32[64,512]{1,0:T(8,128)S(1)}, f32[64,512]{1,0:T(8,128)}, u32[]{:S(2)}, u32[]{:S(2)}) collective-permute-start(f32[64,512]{1,0:T(8,128)S(1)} %get-tuple-element.49), channel_id=1, source_target_pairs={{0,12},{2,14},{4,0},{6,2},{8,4},{10,6},{12,8},{14,10},{1,13},{3,15... | collective-permute-start | bytes 393224 | tf_op jit(solution)/shard_map/ppermute | solution.py:598
  15.0 14.1 %collective-permute-start.5 = (f32[64,512]{1,0:T(8,128)S(1)}, f32[64,512]{1,0:T(8,128)}, u32[]{:S(2)}, u32[]{:S(2)}) collective-permute-start(f32[64,512]{1,0:T(8,128)S(1)} %get-tuple-element.50), channel_id=1, source_target_pairs={{0,8},{2,10},{4,12},{6,14},{8,0},{10,2},{12,4},{14,6},{1,9},{3,11}... | collective-permute-start | bytes 393224 | tf_op jit(solution)/shard_map/ppermute | solution.py:598
  18.4 22.6 %copy-start.21 = (bf16[16,4096]{1,0:T(8,128)(2,1)}, bf16[16,4096]{1,0:T(8,128)(2,1)S(1)}, u32[]{:S(2)}) copy-start(bf16[16,4096]{1,0:T(8,128)(2,1)S(1)} %convert_element_type.31.vectors_ref) | copy-start | bytes 393220
  18.5 13.2 %collective-permute-start.3 = (bf16[16,1024]{1,0:T(8,128)(2,1)S(1)}, bf16[16,1024]{1,0:T(8,128)(2,1)S(1)}, u32[]{:S(2)}, u32[]{:S(2)}) collective-permute-start(bf16[16,1024]{1,0:T(8,128)(2,1)S(1)} %get-tuple-element.65), channel_id=1, source_target_pairs={{0,4},{2,6},{4,8},{6,10},{8,12},{10,14},{12,0},{14,2},{1,5},{3,7},... | collective-permute-start | bytes 98312 | tf_op jit(solution)/shard_map/ppermute | solution.py:598
  20.1 11.6 %collective-permute-start.2 = (bf16[16,1024]{1,0:T(8,128)(2,1)S(1)}, bf16[16,1024]{1,0:T(8,128)(2,1)S(1)}, u32[]{:S(2)}, u32[]{:S(2)}) collective-permute-start(bf16[16,1024]{1,0:T(8,128)(2,1)S(1)} %get-tuple-element.66), channel_id=1, source_target_pairs={{0,8},{2,10},{4,12},{6,14},{8,0},{10,2},{12,4},{14,6},{1,9},{3,11}... | collective-permute-start | bytes 98312 | tf_op jit(solution)/shard_map/ppermute | solution.py:598
  20.5 11.2 %collective-permute-start.1 = (bf16[16,1024]{1,0:T(8,128)(2,1)S(1)}, bf16[16,1024]{1,0:T(8,128)(2,1)S(1)}, u32[]{:S(2)}, u32[]{:S(2)}) collective-permute-start(bf16[16,1024]{1,0:T(8,128)(2,1)S(1)} %get-tuple-element.67), channel_id=1, source_target_pairs={{0,12},{2,14},{4,0},{6,2},{8,4},{10,6},{12,8},{14,10},{1,13},{3,15... | collective-permute-start | bytes 98312 | tf_op jit(solution)/shard_map/ppermute | solution.py:598
  30.1 5.3 %collective-permute-start.7 = (f32[64,512]{1,0:T(8,128)S(1)}, f32[64,512]{1,0:T(8,128)S(1)}, u32[]{:S(2)}, u32[]{:S(2)}) collective-permute-start(f32[64,512]{1,0:T(8,128)S(1)} %add_add_fusion), channel_id=1, source_target_pairs={{0,2},{2,0},{4,6},{6,4},{8,10},{10,8},{12,14},{14,12},{1,3},{3,1},... | collective-permute-start | bytes 393224 | tf_op jit(solution)/shard_map/ppermute | solution.py:594
  35.5 12.1 %collective-permute-start.10 = (f32[64,512]{1,0:T(8,128)S(1)}, f32[64,512]{1,0:T(8,128)S(1)}, u32[]{:S(2)}, u32[]{:S(2)}) collective-permute-start(f32[64,512]{1,0:T(8,128)S(1)} %add.290.refs_1_), channel_id=1, source_target_pairs={{0,4},{2,6},{4,8},{6,10},{8,12},{10,14},{12,0},{14,2},{1,5},{3,7},... | collective-permute-start | bytes 393224 | tf_op jit(solution)/shard_map/ppermute | solution.py:598
  35.6 12.1 %collective-permute-start.9 = (f32[64,512]{1,0:T(8,128)S(1)}, f32[64,512]{1,0:T(8,128)S(1)}, u32[]{:S(2)}, u32[]{:S(2)}) collective-permute-start(f32[64,512]{1,0:T(8,128)S(1)} %add.290.refs_1_), channel_id=1, source_target_pairs={{0,8},{2,10},{4,12},{6,14},{8,0},{10,2},{12,4},{14,6},{1,9},{3,11}... | collective-permute-start | bytes 393224 | tf_op jit(solution)/shard_map/ppermute | solution.py:598
  38.0 9.7 %collective-permute-start.8 = (f32[64,512]{1,0:T(8,128)S(1)}, f32[64,512]{1,0:T(8,128)S(1)}, u32[]{:S(2)}, u32[]{:S(2)}) collective-permute-start(f32[64,512]{1,0:T(8,128)S(1)} %add.290.refs_1_), channel_id=1, source_target_pairs={{0,12},{2,14},{4,0},{6,2},{8,4},{10,6},{12,8},{14,10},{1,13},{3,15... | collective-permute-start | bytes 393224 | tf_op jit(solution)/shard_map/ppermute | solution.py:598
  39.4 9.4 %collective-permute-start.11 = (bf16[64,768]{1,0:T(8,128)(2,1)S(1)}, bf16[64,768]{1,0:T(8,128)(2,1)S(1)}, u32[]{:S(2)}, u32[]{:S(2)}) collective-permute-start(bf16[64,768]{1,0:T(8,128)(2,1)S(1)} %broadcast_select_fusion.1.refs_0_), channel_id=1, source_target_pairs={{0,2},{2,0},{4,6},{6,4},{8,10},{10,8},{12,14},{14,12},{1,3},{3,1},... | collective-permute-start | bytes 294920 | tf_op jit(solution)/shard_map/ppermute | solution.py:594
  48.8 21.6 %copy-start.9 = (f32[256,512]{1,0:T(8,128)}, f32[256,512]{1,0:T(8,128)S(1)}, u32[]{:S(2)}) copy-start(f32[256,512]{1,0:T(8,128)S(1)} %pad_maximum_fusion.refs_2_.mine_ref) | copy-start | bytes 1572868
  48.8 14.9 %copy-start.14 = (bf16[64,768]{1,0:T(8,128)(2,1)}, bf16[64,768]{1,0:T(8,128)(2,1)S(1)}, u32[]{:S(2)}) copy-start(bf16[64,768]{1,0:T(8,128)(2,1)S(1)} %collective-permute-done.11.refs_3_.came_ref) | copy-start | bytes 294916
  48.9 20.4 %collective-permute-start.12 = (bf16[256,1280]{1,0:T(8,128)(2,1)S(1)}, bf16[256,1280]{1,0:T(8,128)(2,1)S(1)}, u32[]{:S(2)}, u32[]{:S(2)}) collective-permute-start(bf16[256,1280]{1,0:T(8,128)(2,1)S(1)} %get-tuple-element.24.refs_0_), channel_id=1, source_target_pairs={{0,4},{4,8},{8,12},{12,14},{14,10},{10,6},{6,2},{2,0},{1,5},{5,9},... | collective-permute-start | bytes 1966088 | tf_op jit(solution)/shard_map/ppermute | solution.py:712
  51.1 12.7 %collective-permute-start.15 = (bf16[256,1024]{1,0:T(8,128)(2,1)S(1)}, bf16[256,1024]{1,0:T(8,128)(2,1)S(1)}, u32[]{:S(2)}, u32[]{:S(2)}) collective-permute-start(bf16[256,1024]{1,0:T(8,128)(2,1)S(1)} %get-tuple-element.25), channel_id=1, source_target_pairs={{0,2},{4,0},{8,4},{12,8},{14,12},{10,14},{6,10},{2,6},{1,3},{5,1},... | collective-permute-start | bytes 1572872 | tf_op jit(solution)/shard_map/ppermute | solution.py:713
  67.7 49.9 %collective-permute-start.16 = (bf16[256,2304]{1,0:T(8,128)(2,1)}, bf16[256,2304]{1,0:T(8,128)(2,1)}, u32[]{:S(2)}, u32[]{:S(2)}) collective-permute-start(bf16[256,2304]{1,0:T(8,128)(2,1)} %add_terms.9.refs_1_), channel_id=1, source_target_pairs={{0,2},{4,0},{8,4},{12,8},{14,12},{10,14},{6,10},{2,6},{1,3},{5,1},... | collective-permute-start | bytes 3538952 | tf_op jit(solution)/shard_map/ppermute | solution.py:723
  69.7 50.8 %collective-permute-start.13 = (bf16[256,2304]{1,0:T(8,128)(2,1)S(1)}, bf16[256,2304]{1,0:T(8,128)(2,1)}, u32[]{:S(2)}, u32[]{:S(2)}) collective-permute-start(bf16[256,2304]{1,0:T(8,128)(2,1)S(1)} %add_terms.8.refs_0_), channel_id=1, source_target_pairs={{0,4},{4,8},{8,12},{12,14},{14,10},{10,6},{6,2},{2,0},{1,5},{5,9},... | collective-permute-start | bytes 3538952 | tf_op jit(solution)/shard_map/ppermute | solution.py:722
  70.4 1.9 collective-permute-start.14
  94.6 23.0 %slice-start = ((s8[4718592]{0:T(1024)(128)(4,1)}), s8[4194304]{0:T(1024)(128)(4,1)S(1)}, s32[]{:S(2)}) async-start(s8[4718592]{0:T(1024)(128)(4,1)} %bitcast.23), calls=%async_computation | async-start | bytes 8388608
  94.6 21.4 %copy-start.19 = (s32[2]{0:T(128)S(1)}, s32[2]{0:T(128)}, u32[]{:S(2)}) copy-start(s32[2]{0:T(128)} %pad_add_fusion.1.place_ref) | copy-start | bytes 28
  94.6 23.0 %slice-start.1 = ((s8[4718592]{0:T(1024)(128)(4,1)}), s8[524288]{0:T(1024)(128)(4,1)S(1)}, s32[]{:S(2)}) async-start(s8[4718592]{0:T(1024)(128)(4,1)} %bitcast.23), calls=%async_computation.1 | async-start | bytes 1048576
  102.7 8.5 %collective-permute-start.17 = (bf16[2,128,256]{2,1,0:T(8,128)(2,1)}, bf16[2,128,256]{2,1,0:T(8,128)(2,1)S(1)}, u32[]{:S(2)}, u32[]{:S(2)}) collective-permute-start(bf16[2,128,256]{2,1,0:T(8,128)(2,1)} %get-tuple-element.28), channel_id=1, source_target_pairs={{0,4},{2,6},{4,8},{6,10},{8,12},{10,14},{12,0},{14,2},{1,5},{3,7},... | collective-permute-start | bytes 393224 | tf_op jit(solution)/shard_map/ppermute | solution.py:598
  104.7 11.3 %collective-permute-start.18 = (bf16[2,128,256]{2,1,0:T(8,128)(2,1)}, bf16[2,128,256]{2,1,0:T(8,128)(2,1)S(1)}, u32[]{:S(2)}, u32[]{:S(2)}) collective-permute-start(bf16[2,128,256]{2,1,0:T(8,128)(2,1)} %get-tuple-element.29), channel_id=1, source_target_pairs={{0,8},{2,10},{4,12},{6,14},{8,0},{10,2},{12,4},{14,6},{1,9},{3,11}... | collective-permute-start | bytes 393224 | tf_op jit(solution)/shard_map/ppermute | solution.py:598
  104.7 11.3 %collective-permute-start.19 = (bf16[2,128,256]{2,1,0:T(8,128)(2,1)}, bf16[2,128,256]{2,1,0:T(8,128)(2,1)S(1)}, u32[]{:S(2)}, u32[]{:S(2)}) collective-permute-start(bf16[2,128,256]{2,1,0:T(8,128)(2,1)} %get-tuple-element.30), channel_id=1, source_target_pairs={{0,12},{2,14},{4,0},{6,2},{8,4},{10,6},{12,8},{14,10},{1,13},{3,15... | collective-permute-start | bytes 393224 | tf_op jit(solution)/shard_map/ppermute | solution.py:598
  122.3 28.7 %collective-permute-start.20 = (bf16[256,2304]{1,0:T(8,128)(2,1)S(1)}, bf16[256,2304]{1,0:T(8,128)(2,1)}, u32[]{:S(2)}, u32[]{:S(2)}) collective-permute-start(bf16[256,2304]{1,0:T(8,128)(2,1)S(1)} %get-tuple-element.32.refs_0_), channel_id=1, source_target_pairs={{0,4},{4,8},{8,12},{12,14},{14,10},{10,6},{6,2},{2,0},{1,5},{5,9},... | collective-permute-start | bytes 3538952 | tf_op jit(solution)/shard_map/ppermute | solution.py:722
  125.6 31.5 %collective-permute-start.22 = (bf16[256,2304]{1,0:T(8,128)(2,1)}, bf16[256,2304]{1,0:T(8,128)(2,1)}, u32[]{:S(2)}, u32[]{:S(2)}) collective-permute-start(bf16[256,2304]{1,0:T(8,128)(2,1)} %get-tuple-element.33), channel_id=1, source_target_pairs={{0,2},{4,0},{8,4},{12,8},{14,12},{10,14},{6,10},{2,6},{1,3},{5,1},... | collective-permute-start | bytes 3538952 | tf_op jit(solution)/shard_map/ppermute | solution.py:723
  154.5 18.2 %collective-permute-start.21 = (bf16[256,1280]{1,0:T(8,128)(2,1)S(1)}, bf16[256,1280]{1,0:T(8,128)(2,1)}, u32[]{:S(2)}, u32[]{:S(2)}) collective-permute-start(bf16[256,1280]{1,0:T(8,128)(2,1)S(1)} %add_terms.12.refs_1_), channel_id=1, source_target_pairs={{0,4},{4,8},{8,12},{12,14},{14,10},{10,6},{6,2},{2,0},{1,5},{5,9},... | collective-permute-start | bytes 1966088 | tf_op jit(solution)/shard_map/ppermute | solution.py:742
  158.6 17.8 %collective-permute-start.23 = (bf16[256,1280]{1,0:T(8,128)(2,1)S(1)}, bf16[256,1280]{1,0:T(8,128)(2,1)}, u32[]{:S(2)}, u32[]{:S(2)}) collective-permute-start(bf16[256,1280]{1,0:T(8,128)(2,1)S(1)} %add_terms.13.refs_2_), channel_id=1, source_target_pairs={{0,2},{4,0},{8,4},{12,8},{14,12},{10,14},{6,10},{2,6},{1,3},{5,1},... | collective-permute-start | bytes 1966088 | tf_op jit(solution)/shard_map/ppermute | solution.py:742
  161.1 25.0 %collective-permute-start.24 = (bf16[256,1024]{1,0:T(8,128)(2,1)}, bf16[256,1024]{1,0:T(8,128)(2,1)}, u32[]{:S(2)}, u32[]{:S(2)}) collective-permute-start(bf16[256,1024]{1,0:T(8,128)(2,1)} %add_terms.14), channel_id=1, source_target_pairs={{0,4},{4,8},{8,12},{12,14},{14,10},{10,6},{6,2},{2,0},{1,5},{5,9},... | collective-permute-start | bytes 1572872 | tf_op jit(solution)/shard_map/ppermute | solution.py:743
  165.3 24.9 %collective-permute-start.25 = (bf16[256,1024]{1,0:T(8,128)(2,1)}, bf16[256,1024]{1,0:T(8,128)(2,1)}, u32[]{:S(2)}, u32[]{:S(2)}) collective-permute-start(bf16[256,1024]{1,0:T(8,128)(2,1)} %add_terms.15), channel_id=1, source_target_pairs={{0,2},{4,0},{8,4},{12,8},{14,12},{10,14},{6,10},{2,6},{1,3},{5,1},... | collective-permute-start | bytes 1572872 | tf_op jit(solution)/shard_map/ppermute | solution.py:743
  178.5 11.7 %copy-start.3 = (bf16[3,256,2304]{2,1,0:T(8,128)(2,1)S(1)}, bf16[3,256,2304]{2,1,0:T(8,128)(2,1)}, u32[]{:S(2)}) copy-start(bf16[3,256,2304]{2,1,0:T(8,128)(2,1)} %window_terms.5.terms_ref) | copy-start | bytes 10616836
  180.5 19.6 %collective-permute-start.26 = (bf16[2,256,256]{2,1,0:T(8,128)(2,1)S(1)}, bf16[2,256,256]{2,1,0:T(8,128)(2,1)S(1)}, u32[]{:S(2)}, u32[]{:S(2)}) collective-permute-start(bf16[2,256,256]{2,1,0:T(8,128)(2,1)S(1)} %get-tuple-element.36), channel_id=1, source_target_pairs={{0,12},{4,14},{8,10},{12,6},{14,2},{10,0},{6,4},{2,8},{1,13},{5,15... | collective-permute-start | bytes 786440 | tf_op jit(solution)/shard_map/ppermute | solution.py:753
  181.8 25.6 %collective-permute-start.27 = (bf16[2,256,256]{2,1,0:T(8,128)(2,1)S(1)}, bf16[2,256,256]{2,1,0:T(8,128)(2,1)S(1)}, u32[]{:S(2)}, u32[]{:S(2)}) collective-permute-start(bf16[2,256,256]{2,1,0:T(8,128)(2,1)S(1)} %get-tuple-element.37), channel_id=1, source_target_pairs={{0,6},{4,2},{8,0},{12,4},{14,8},{10,12},{6,14},{2,10},{1,7},{5,3},... | collective-permute-start | bytes 786440 | tf_op jit(solution)/shard_map/ppermute | solution.py:753
  182.3 17.2 %collective-permute-start.29 = (bf16[1,256,256]{2,1,0:T(8,128)(2,1)S(1)}, bf16[1,256,256]{2,1,0:T(8,128)(2,1)S(1)}, u32[]{:S(2)}, u32[]{:S(2)}) collective-permute-start(bf16[1,256,256]{2,1,0:T(8,128)(2,1)S(1)} %get-tuple-element.39), channel_id=1, source_target_pairs={{0,14},{4,10},{8,6},{12,2},{14,0},{10,4},{6,8},{2,12},{1,15},{5,11... | collective-permute-start | bytes 393224 | tf_op jit(solution)/shard_map/ppermute | solution.py:753
  186.0 21.3 %copy-start.13 = (f32[512,128]{1,0:T(8,128)S(1)}, f32[512,128]{1,0:T(8,128)}, u32[]{:S(2)}) copy-start(f32[512,128]{1,0:T(8,128)} %get-tuple-element.26.solved_ref) | copy-start | bytes 786436
  186.1 21.3 %copy-start.17 = (f32[128,256]{1,0:T(8,128)S(1)}, f32[128,256]{1,0:T(8,128)}, u32[]{:S(2)}) copy-start(f32[128,256]{1,0:T(8,128)} %copy-done.16) | copy-start | bytes 393220
  186.1 21.3 %copy-start.18 = (f32[128,128]{1,0:T(8,128)S(1)}, f32[128,128]{1,0:T(8,128)}, u32[]{:S(2)}) copy-start(f32[128,128]{1,0:T(8,128)} %get-tuple-element.40.first_ref) | copy-start | bytes 196612
  186.1 21.3 %copy-start.20 = (s32[2]{0:T(128)S(1)}, s32[2]{0:T(128)}, u32[]{:S(2)}) copy-start(s32[2]{0:T(128)} %pad_add_fusion.1.place_ref) | copy-start | bytes 28
  186.1 9.2 %collective-permute-start.31 = (bf16[128,256]{1,0:T(8,128)(2,1)S(1)}, bf16[128,256]{1,0:T(8,128)(2,1)S(1)}, u32[]{:S(2)}, u32[]{:S(2)}) collective-permute-start(bf16[128,256]{1,0:T(8,128)(2,1)S(1)} %get-tuple-element.31.refs_2_), channel_id=1, source_target_pairs={{0,2},{2,0},{4,6},{6,4},{8,10},{10,8},{12,14},{14,12},{1,3},{3,1},... | collective-permute-start | bytes 196616 | tf_op jit(solution)/shard_map/ppermute | solution.py:594
  191.9 22.7 %collective-permute-start.28 = (bf16[2,256,256]{2,1,0:T(8,128)(2,1)S(1)}, bf16[2,256,256]{2,1,0:T(8,128)(2,1)S(1)}, u32[]{:S(2)}, u32[]{:S(2)}) collective-permute-start(bf16[2,256,256]{2,1,0:T(8,128)(2,1)S(1)} %get-tuple-element.38), channel_id=1, source_target_pairs={{0,2},{4,0},{8,4},{12,8},{14,12},{10,14},{6,10},{2,6},{1,3},{5,1},... | collective-permute-start | bytes 786440 | tf_op jit(solution)/shard_map/ppermute | solution.py:753
  208.6 7.9 %collective-permute-start.32 = (f32[64,128]{1,0:T(8,128)S(1)}, f32[64,128]{1,0:T(8,128)S(1)}, u32[]{:S(2)}, u32[]{:S(2)}) collective-permute-start(f32[64,128]{1,0:T(8,128)S(1)} %slice_select_fusion), channel_id=1, source_target_pairs={{0,8},{2,10},{4,12},{6,14},{8,0},{10,2},{12,4},{14,6},{1,9},{3,11}... | collective-permute-start | bytes 98312 | tf_op jit(solution)/shard_map/ppermute | solution.py:763
  216.5 3.8 %collective-permute-start.33 = (f32[32,128]{1,0:T(8,128)S(1)}, f32[32,128]{1,0:T(8,128)S(1)}, u32[]{:S(2)}, u32[]{:S(2)}) collective-permute-start(f32[32,128]{1,0:T(8,128)S(1)} %slice_select_fusion.1), channel_id=1, source_target_pairs={{0,4},{2,6},{4,0},{6,2},{8,12},{10,14},{12,8},{14,10},{1,5},{3,7},... | collective-permute-start | bytes 49160 | tf_op jit(solution)/shard_map/ppermute | solution.py:763
  216.6 8.6 %copy-start.28 = (s32[256]{0:T(256)S(1)}, s32[256]{0:T(256)}, u32[]{:S(2)}) copy-start(s32[256]{0:T(256)} %param.16) | copy-start | bytes 3076
  218.3 7.8 %collective-permute-start.30 = (bf16[8,256,256]{2,1,0:T(8,128)(2,1)}, bf16[8,256,256]{2,1,0:T(8,128)(2,1)S(1)}, u32[]{:S(2)}, u32[]{:S(2)}) collective-permute-start(bf16[8,256,256]{2,1,0:T(8,128)(2,1)} %for_sibling.1), channel_id=1, source_target_pairs={{0,1},{1,0},{2,3},{3,2},{4,5},{5,4},{6,7},{7,6},{8,9},{9,8},{10,11... | collective-permute-start | bytes 3145736 | tf_op jit(solution)/shard_map/ppermute | solution.py:770
  220.3 3.7 %collective-permute-start.34 = (f32[16,128]{1,0:T(8,128)S(1)}, f32[16,128]{1,0:T(8,128)S(1)}, u32[]{:S(2)}, u32[]{:S(2)}) collective-permute-start(f32[16,128]{1,0:T(8,128)S(1)} %slice_select_fusion.2), channel_id=1, source_target_pairs={{0,2},{2,0},{4,6},{6,4},{8,10},{10,8},{12,14},{14,12},{1,3},{3,1},... | collective-permute-start | bytes 24584 | tf_op jit(solution)/shard_map/ppermute | solution.py:763
  224.1 1.2 collective-permute-start.35
  (21 other events, 59.7 us)
where the time goes:
time: 234 us; the launch traced here: 231 us
  Pallas kernels  83.8 us (36%)
  waiting for transfers between devices  66.9 us (29%)
  starting transfers between devices  52.5 us (22%)
  local copies, waits for them, and re-layouts  12.9 us (6%)
  matrix products  9.28 us (4%)
  other arithmetic  4.1 us (2%)
    pallas_call x3, Pallas kernels, window_terms(): pl.pallas_call(kernel, grid_spec=pltpu.PrefetchScalarGridSpec(num_scalar_...  29.7 us
    pallas_call x1, Pallas kernels, solve(): pl.pallas_call(kernel, in_specs=[pl.BlockSpec(memory_space=pltpu.SMEM)] +...  21.5 us
    ppermute x12, starting transfers between devices, far_shift(): lax.ppermute(value, 'dp', [(index, (index + 2 * step) % count) for index...  20.2 us
    ppermute x2, waiting for transfers between devices, local(): came_ahead = lax.ppermute(going, 'dp', ahead)  14.7 us
    pallas_call x8, Pallas kernels, add_terms(): pl.pallas_call(kernel, in_specs=[MAIN] + [FAST] * len(arrived) + [ANYWHER...  13.9 us
    ppermute x12, waiting for transfers between devices, far_shift(): lax.ppermute(value, 'dp', [(index, (index + 2 * step) % count) for index...  13.5 us
    ppermute x4, waiting for transfers between devices, local(): lax.ppermute(turned[offset], 'dp', ring.shift(offset))  12.1 us
    unnamed x67, local copies, waits for them, and re-layouts  10.8 us
  transfers between devices with their start and end apart: 36, of which 17 were waited for; matrix products, arithmetic and copies ran while one was open for 4% of the time, Pallas kernels for 34%

commit v1 on v0

--- a/solution.py
+++ b/solution.py
@@ -178,7 +178,7 @@
 
     return pl.pallas_call(
         kernel,
-        in_specs=[MAIN] + [FAST] * len(arrived) + [ANYWHERE] * len(after),
+        in_specs=[ANYWHERE] + [FAST] * len(arrived) + [ANYWHERE] * len(after),
         out_specs=FAST,
         out_shape=jax.ShapeDtypeStruct((group, count * group), jnp.bfloat16),
         scratch_shapes=[pltpu.VMEM((group, count * group), jnp.bfloat16), pltpu.SemaphoreType.DMA],
@@ -227,7 +227,7 @@
     sizes = [count] + [blocks for _, blocks, _ in chips]
     return pl.pallas_call(
         kernel,
-        in_specs=[MAIN, FAST, FAST] + [ANYWHERE] * len(after),
+        in_specs=[ANYWHERE, FAST, FAST] + [ANYWHERE] * len(after),
         out_specs=[FAST] * len(sizes),
         out_shape=[jax.ShapeDtypeStruct((size, group, group), jnp.bfloat16) for size in sizes],
         scratch_shapes=[pltpu.VMEM(terms.shape[1:], jnp.bfloat16), pltpu.SemaphoreType.DMA],
@@ -642,6 +642,7 @@
     pairs_count = owners // 2
     first_stored = stored[:, :width]
     corner_rows = lead_dot(lax.dynamic_slice_in_dim(first_stored, t * group, group, 1), first_stored)
+    activations, out_grads, corner_rows = lax.optimization_barrier((activations, out_grads, corner_rows))
     corner_payload = scatter_pairs(corner_rows, pair, owners)
 
     sides = jnp.concatenate(
@@ -721,7 +722,7 @@
     for step in range(half - 2, 0, -1):
         came_ahead = lax.ppermute(going, "dp", ahead)
         came_back = lax.ppermute(coming, "dp", back)
-        own, index, token = (second, 2, [pieces[0]]) if step == half - 2 else (later, later_steps.index(step), [])
+        own, index, token = (second, 2, [pieces[0]]) if step == half - 2 else (later, later_steps.index(step), [away])
         if step == 1:
             far_going = add_terms(own, index, [(came_ahead, 0)], 0, far_count, group, token)
             far_coming = add_terms(own, index + 1, [(came_back, 0)], 0, far_count, group, token)
@@ -734,11 +735,10 @@
             coming = add_terms(own, index + 1, [(came_back, 0)], 0, total, group, token)
             token = [going, coming]
         if step == half - 2:
+            later = terms_of(later_steps, [slots], token)[0]
             came = [pieces[0]] + [far_shift(pieces[index], index, owners) for index in range(1, pairs_count)]
-            terms, away = sum_pieces(place, came)
+            terms, away = sum_pieces(place, came, [later])
             terms_other = pair_swap(away, owners)
-            going, coming = gate([going, coming], [away])
-            later = terms_of(later_steps, [slots], [going])[0]
     far_sums = [lax.ppermute(far_going, "dp", ahead), lax.ppermute(far_coming, "dp", back)]
     near_sums = [lax.ppermute(near_going, "dp", ahead), lax.ppermute(near_coming, "dp", back)]
 
@@ -754,8 +754,12 @@
         for offset in [half] + ring.offsets
     }
     came = [shifted[offset] for offset in ring.offsets + [half]]
-    early = [shifted[offset] for offset in [half] + ring.offsets[:split]]
-    pairs = pair_products(place, own_cols, first_pairs, terms, terms_other, solved, early)
+    blocks = jnp.concatenate([far[0], near[0]] + came, axis=0)
+    send_table, final_table = assembly_tables(ring, far_slots + near_slots, d, t)
+    send = for_sibling(send_table, blocks, group)
+    other = lax.ppermute(send, "tensor", SWAP)
+
+    pairs = pair_products(place, own_cols, first_pairs, terms, terms_other, solved, [send])
     bit = owners // 2
     while bit >= 1:
         kept_rows = jnp.where((d & bit) == 0, pairs[: pairs.shape[0] // 2], pairs[pairs.shape[0] // 2 :])
@@ -765,9 +769,6 @@
     pairs = pairs + lax.ppermute(pairs, "tensor", SWAP)
     chosen = (query_ids[:, None] == jnp.arange(all_examples, dtype=jnp.int32)[None, :]).astype(jnp.float32)
     scores = lax.dot_general(chosen, pairs, (((1,), (1,)), ((), ())), precision=EXACT, preferred_element_type=jnp.float32) / R
-    blocks = jnp.concatenate([far[0], near[0]] + came, axis=0)
-    send_table, final_table = assembly_tables(ring, far_slots + near_slots, d, t)
-    other = lax.ppermute(for_sibling(send_table, blocks, group), "tensor", SWAP)
     return finish(place, final_table, blocks, other, half, group), scores
 
 

time: 234 us -> 226 us (0.966)
  waiting for transfers between devices: 66.9 us -> 52.9 us
  starting transfers between devices: 52.5 us -> 58.5 us
  local copies, waits for them, and re-layouts: 12.9 us -> 18.2 us
  Pallas kernels: 83.8 us -> 79 us
    ppermute x2, waiting for transfers between devices: 14.7 us -> 0.01 us  [local(): came_ahead = lax.ppermute(going, 'dp', ahead)]
    ppermute x4, starting transfers between devices: 5.56 us -> 17 us  [local(): lax.ppermute(turned[offset], 'dp', ring.shift(offset))]
    ppermute x12, waiting for transfers between devices: 13.5 us -> 22.9 us  [far_shift(): lax.ppermute(value, 'dp', [(index, (index + 2 * step) % count) for index...]
    ppermute x3, waiting for transfers between devices: 6.23 us -> 0.01 us  [pair_swap(): lax.ppermute(value, 'dp', [(index, index ^ 1) for index in range(count)])]
    ppermute x4, waiting for transfers between devices: 12.1 us -> 6.34 us  [local(): lax.ppermute(turned[offset], 'dp', ring.shift(offset))]
    ppermute x1, starting transfers between devices: 0.06 us -> 4.51 us  [local(): lax.ppermute(far_coming, 'dp', back)]
    pallas_call x1, Pallas kernels: 21.5 us -> 17.1 us  [solve(): pl.pallas_call(kernel, in_specs=[pl.BlockSpec(memory_space=pltpu.SMEM)] +...]
    ppermute x3, starting transfers between devices: 7.23 us -> 3.57 us  [pair_swap(): lax.ppermute(value, 'dp', [(index, index ^ 1) for index in range(count)])]
  transfers between devices with their start and end apart: 36 -> 36, of which waited for: 17 -> 19; matrix products, arithmetic and copies ran while one was open for 4% -> 6% of each run, Pallas kernels for 34% -> 33%
where the time goes in v1:
time: 226 us; the launch traced here: 224 us
  Pallas kernels  79 us (35%)
  starting transfers between devices  58.5 us (26%)
  waiting for transfers between devices  52.9 us (23%)
  local copies, waits for them, and re-layouts  18.2 us (8%)
  matrix products  9.91 us (4%)
  other arithmetic  3.79 us (2%)
    pallas_call x3, Pallas kernels, window_terms(): pl.pallas_call(kernel, grid_spec=pltpu.PrefetchScalarGridSpec(num_scalar_...  29.9 us
    ppermute x12, waiting for transfers between devices, far_shift(): lax.ppermute(value, 'dp', [(index, (index + 2 * step) % count) for index...  22.9 us
    ppermute x12, starting transfers between devices, far_shift(): lax.ppermute(value, 'dp', [(index, (index + 2 * step) % count) for index...  17.8 us
    pallas_call x1, Pallas kernels, solve(): pl.pallas_call(kernel, in_specs=[pl.BlockSpec(memory_space=pltpu.SMEM)] +...  17.1 us
    ppermute x4, starting transfers between devices, local(): lax.ppermute(turned[offset], 'dp', ring.shift(offset))  17 us
    unnamed x73, local copies, waits for them, and re-layouts  13.9 us
    pallas_call x8, Pallas kernels, add_terms(): pl.pallas_call(kernel, in_specs=[ANYWHERE] + [FAST] * len(arrived) + [ANY...  13.9 us
    ppermute x3, waiting for transfers between devices, local(): lax.ppermute(sent_rows, 'dp', [(index, index ^ bit) for index in range(ow...  8.88 us
  transfers between devices with their start and end apart: 36, of which 19 were waited for; matrix products, arithmetic and copies ran while one was open for 6% of the time, Pallas kernels for 33%

profile of v1, /device:TPU:0, one launch (start us, length us, event | category | flops | bytes accessed | tf_op | source)
XLA Modules:
  0.0 223.7 jit_solution(2977214602467036282)
XLA Ops:
  0.7 1.8 slice-done.3
  4.8 3.1 %collective-permute-start.4 = (f32[64,512]{1,0:T(8,128)S(1)}, f32[64,512]{1,0:T(8,128)S(1)}, u32[]{:S(2)}, u32[]{:S(2)}) collective-permute-start(f32[64,512]{1,0:T(8,128)S(1)} %get-tuple-element.50), channel_id=1, source_target_pairs={{0,4},{2,6},{4,8},{6,10},{8,12},{10,14},{12,0},{14,2},{1,5},{3,7},... | collective-permute-start | bytes 393224 | tf_op jit(solution)/shard_map/ppermute | solution.py:598
  7.9 2.6 %collective-permute-start.5 = (f32[64,512]{1,0:T(8,128)S(1)}, f32[64,512]{1,0:T(8,128)S(1)}, u32[]{:S(2)}, u32[]{:S(2)}) collective-permute-start(f32[64,512]{1,0:T(8,128)S(1)} %get-tuple-element.52), channel_id=1, source_target_pairs={{0,8},{2,10},{4,12},{6,14},{8,0},{10,2},{12,4},{14,6},{1,9},{3,11}... | collective-permute-start | bytes 393224 | tf_op jit(solution)/shard_map/ppermute | solution.py:598
  11.8 5.9 %fusion.29 = f32[256,64]{0,1:T(8,128)S(1)} fusion(bf16[256,14336]{1,0:T(8,128)(2,1)} %param.10, bf16[14336,64]{0,1:T(8,128)(2,1)} %param.12), kind=kOutput, calls=%fused_computation.118 | convolution fusion | flops 469762048 | bytes 9240576 | tf_op jit(solution)/shard_map/dot_general | solution.py:650
  22.2 1.7 collective-permute-start.2
  24.9 1.7 collective-permute-start.7
  27.2 2.3 %collective-permute-done.3 = bf16[16,1024]{1,0:T(8,128)(2,1)S(1)} collective-permute-done((bf16[16,1024]{1,0:T(8,128)(2,1)S(1)}, bf16[16,1024]{1,0:T(8,128)(2,1)S(1)}, u32[]{:S(2)}, u32[]{:S(2)}) %collective-permute-start.3) | collective-permute-done | bytes 32800 | tf_op jit(solution)/shard_map/ppermute | solution.py:598
  31.7 2.5 %collective-permute-start.8 = (f32[64,512]{1,0:T(8,128)S(1)}, f32[64,512]{1,0:T(8,128)S(1)}, u32[]{:S(2)}, u32[]{:S(2)}) collective-permute-start(f32[64,512]{1,0:T(8,128)S(1)} %add.290.refs_1_), channel_id=1, source_target_pairs={{0,12},{2,14},{4,0},{6,2},{8,4},{10,6},{12,8},{14,10},{1,13},{3,15... | collective-permute-start | bytes 393224 | tf_op jit(solution)/shard_map/ppermute | solution.py:598
  34.8 1.6 collective-permute-start.11
  36.4 6.6 %window_terms.3 = (bf16[1,256,1280]{2,1,0:T(8,128)(2,1)}, bf16[1,256,1024]{2,1,0:T(8,128)(2,1)}) custom-call(s32[2]{0:T(128)} %pad_add_fusion.1.place_ref, s32[1]{0:T(128)} %constant.135.clone.step_ref, bf16[1024,4096]{1,0:T(8,128)(2,1)} %stored_ref.5, bf16[16,4096]{1,0:T(8,128)(2,1)} %copy-done.25, bf16[64,768]{1,0:T(8,128)(2,1)} %copy-done.29, ...), custom_call_target="tpu_custom_call" | custom-call | flops 1000000 | bytes 100000 | tf_op jit(solution)/shard_map/window_terms/pallas_call | solution.py:144
  43.0 1.4 collective-permute-done.9
  45.9 1.8 collective-permute-start.15
  47.6 12.6 %window_terms.4.terms_ref = bf16[4,256,2304]{2,1,0:T(8,128)(2,1)} custom-call(s32[2]{0:T(128)} %pad_add_fusion.1.place_ref, s32[4]{0:T(128)} %constant.136.clone.step_ref, bf16[1024,4096]{1,0:T(8,128)(2,1)} %stored_ref.5, bf16[16,4096]{1,0:T(8,128)(2,1)} %copy-done.25, bf16[256,1280]{1,0:T(8,128)(2,1)} %copy-done.13), custom_call_target="tpu_custom_call" | custom-call | flops 1000000 | bytes 100000 | tf_op jit(solution)/shard_map/window_terms/pallas_call | solution.py:144
  60.3 2.3 %copy-done.7 = bf16[4,256,2304]{2,1,0:T(8,128)(2,1)S(1)} copy-done((bf16[4,256,2304]{2,1,0:T(8,128)(2,1)S(1)}, bf16[4,256,2304]{2,1,0:T(8,128)(2,1)}, u32[]{:S(2)}) %copy-start.7) | copy-done | bytes 4718616
  63.0 1.6 collective-permute-start.16
  66.8 1.9 collective-permute-done.14.other_ref
  69.5 17.1 %solve.1 = (f32[512,128]{1,0:T(8,128)}, f32[128,128]{1,0:T(8,128)}) custom-call(s32[2]{0:T(128)} %pad_add_fusion.1.place_ref, f32[256,512]{1,0:T(8,128)} %copy-done.10, f32[256,512]{1,0:T(8,128)} %copy-done.28, bf16[64,768]{1,0:T(8,128)(2,1)} %get-tuple-element.44.kept_ref, bf16[64,768]{1,0:T(8,128)(2,1)} %copy-done.17, bf16[256,2304]{1,0:T(8,128)(2,1)} %add_terms.8.refs_0_, ...), custom_call_target="tpu_custom_call" | custom-call | flops 1000000 | bytes 100000 | tf_op jit(solution)/shard_map/solve/pallas_call | solution.py:358
  86.7 8.1 %spread_back.1 = (bf16[2,128,256]{2,1,0:T(8,128)(2,1)}, bf16[2,128,256]{2,1,0:T(8,128)(2,1)}, bf16[2,128,256]{2,1,0:T(8,128)(2,1)}, bf16[2,128,256]{2,1,0:T(8,128)(2,1)}) custom-call(s32[2]{0:T(128)} %pad_add_fusion.1.place_ref, bf16[1024,4096]{1,0:T(8,128)(2,1)} %stored_ref.5, f32[512,128]{1,0:T(8,128)} %get-tuple-element.30.solved_ref, ...), custom_call_target="tpu_custom_call" | custom-call | flops 1000000 | bytes 100000 | tf_op jit(solution)/shard_map/spread_back/pallas_call | solution.py:396
  95.6 1.8 add_terms.11.refs_1_
  97.4 1.6 collective-permute-start.22
  99.0 2.8 %add_terms.10.refs_0_ = bf16[256,2304]{1,0:T(8,128)(2,1)} custom-call(bf16[4,256,2304]{2,1,0:T(8,128)(2,1)S(1)} %bitcast.24, bf16[256,2304]{1,0:T(8,128)(2,1)} %collective-permute-done.13.refs_0_, bf16[2,128,256]{2,1,0:T(8,128)(2,1)S(1)} %copy-done.14), custom_call_target="tpu_custom_call" | custom-call | flops 1000000 | bytes 100000 | tf_op jit(solution)/shard_map/add_terms/pallas_call | solution.py:179
  102.7 2.6 %collective-permute-start.19 = (bf16[2,128,256]{2,1,0:T(8,128)(2,1)}, bf16[2,128,256]{2,1,0:T(8,128)(2,1)S(1)}, u32[]{:S(2)}, u32[]{:S(2)}) collective-permute-start(bf16[2,128,256]{2,1,0:T(8,128)(2,1)} %get-tuple-element.33), channel_id=1, source_target_pairs={{0,8},{2,10},{4,12},{6,14},{8,0},{10,2},{12,4},{14,6},{1,9},{3,11}... | collective-permute-start | bytes 393224 | tf_op jit(solution)/shard_map/ppermute | solution.py:598
  106.5 10.7 %window_terms.5.refs_4_.terms_ref = bf16[3,256,2304]{2,1,0:T(8,128)(2,1)} custom-call(s32[2]{0:T(128)} %pad_add_fusion.1.place_ref, s32[3]{0:T(128)} %constant.137.clone.step_ref, bf16[1024,4096]{1,0:T(8,128)(2,1)} %stored_ref.5, bf16[16,4096]{1,0:T(8,128)(2,1)} %copy-done.25, bf16[256,2304]{1,0:T(8,128)(2,1)} %add_terms.10.refs_0_, bf16[256,2304]{1,0:T(8,128)(2,1)} %copy-done.8), custom_call_target="tpu_custom_call" | custom-call | flops 1000000 | bytes 100000 | tf_op jit(solution)/shard_map/window_terms/pallas_call | solution.py:144
  117.3 14.6 %collective-permute-done.18.refs_1_ = bf16[2,128,256]{2,1,0:T(8,128)(2,1)S(1)} collective-permute-done((bf16[2,128,256]{2,1,0:T(8,128)(2,1)}, bf16[2,128,256]{2,1,0:T(8,128)(2,1)S(1)}, u32[]{:S(2)}, u32[]{:S(2)}) %collective-permute-start.18) | collective-permute-done | bytes 131104 | tf_op jit(solution)/shard_map/ppermute | solution.py:598
  131.9 2.9 %collective-permute-done.19.refs_2_ = bf16[2,128,256]{2,1,0:T(8,128)(2,1)S(1)} collective-permute-done((bf16[2,128,256]{2,1,0:T(8,128)(2,1)}, bf16[2,128,256]{2,1,0:T(8,128)(2,1)S(1)}, u32[]{:S(2)}, u32[]{:S(2)}) %collective-permute-start.19) | collective-permute-done | bytes 131104 | tf_op jit(solution)/shard_map/ppermute | solution.py:598
  136.4 2.0 copy-done.1
  141.4 1.5 add_terms.13.refs_2_
  142.9 4.5 %collective-permute-start.23 = (bf16[256,1280]{1,0:T(8,128)(2,1)S(1)}, bf16[256,1280]{1,0:T(8,128)(2,1)}, u32[]{:S(2)}, u32[]{:S(2)}) collective-permute-start(bf16[256,1280]{1,0:T(8,128)(2,1)S(1)} %add_terms.13.refs_2_), channel_id=1, source_target_pairs={{0,2},{4,0},{8,4},{12,8},{14,12},{10,14},{6,10},{2,6},{1,3},{5,1},... | collective-permute-start | bytes 1966088 | tf_op jit(solution)/shard_map/ppermute | solution.py:742
  147.4 1.5 add_terms.12.refs_1_
  149.1 2.2 %add_terms.15 = bf16[256,1024]{1,0:T(8,128)(2,1)} custom-call(bf16[3,256,2304]{2,1,0:T(8,128)(2,1)S(1)} %copy-done.2, bf16[256,2304]{1,0:T(8,128)(2,1)} %collective-permute-done.22.refs_0_, bf16[256,1280]{1,0:T(8,128)(2,1)S(1)} %add_terms.12.refs_1_, bf16[256,1280]{1,0:T(8,128)(2,1)S(1)} %add_terms.13.refs_2_), custom_call_target="tpu_custom_call" | custom-call | flops 1000000 | bytes 100000 | tf_op jit(solution)/shard_map/add_terms/pallas_call | solution.py:179
  151.3 2.0 collective-permute-start.25
  153.4 2.2 add_terms.14
  156.6 6.0 %collective-permute-done.23.back_ref = bf16[256,1280]{1,0:T(8,128)(2,1)} collective-permute-done((bf16[256,1280]{1,0:T(8,128)(2,1)S(1)}, bf16[256,1280]{1,0:T(8,128)(2,1)}, u32[]{:S(2)}, u32[]{:S(2)}) %collective-permute-start.23) | collective-permute-done | bytes 655392 | tf_op jit(solution)/shard_map/ppermute | solution.py:742
  162.6 4.1 %collective-permute-done.21.ahead_ref = bf16[256,1280]{1,0:T(8,128)(2,1)} collective-permute-done((bf16[256,1280]{1,0:T(8,128)(2,1)S(1)}, bf16[256,1280]{1,0:T(8,128)(2,1)}, u32[]{:S(2)}, u32[]{:S(2)}) %collective-permute-start.21) | collective-permute-done | bytes 655392 | tf_op jit(solution)/shard_map/ppermute | solution.py:742
  166.7 2.0 copy-done.3
  168.7 2.0 close_window.2
  170.7 2.0 collective-permute-start.26
  173.0 3.3 %collective-permute-start.27 = (bf16[2,256,256]{2,1,0:T(8,128)(2,1)S(1)}, bf16[2,256,256]{2,1,0:T(8,128)(2,1)S(1)}, u32[]{:S(2)}, u32[]{:S(2)}) collective-permute-start(bf16[2,256,256]{2,1,0:T(8,128)(2,1)S(1)} %get-tuple-element.39), channel_id=1, source_target_pairs={{0,6},{4,2},{8,0},{12,4},{14,8},{10,12},{6,14},{2,10},{1,7},{5,3},... | collective-permute-start | bytes 786440 | tf_op jit(solution)/shard_map/ppermute | solution.py:753
  177.4 1.7 close_window.3
  179.1 10.5 %collective-permute-start.28 = (bf16[2,256,256]{2,1,0:T(8,128)(2,1)S(1)}, bf16[2,256,256]{2,1,0:T(8,128)(2,1)S(1)}, u32[]{:S(2)}, u32[]{:S(2)}) collective-permute-start(bf16[2,256,256]{2,1,0:T(8,128)(2,1)S(1)} %get-tuple-element.40), channel_id=1, source_target_pairs={{0,2},{4,0},{8,4},{12,8},{14,12},{10,14},{6,10},{2,6},{1,3},{5,1},... | collective-permute-start | bytes 786440 | tf_op jit(solution)/shard_map/ppermute | solution.py:753
  190.9 2.0 collective-permute-done.27
  193.5 3.8 %collective-permute-done.29 = bf16[1,256,256]{2,1,0:T(8,128)(2,1)S(1)} collective-permute-done((bf16[1,256,256]{2,1,0:T(8,128)(2,1)S(1)}, bf16[1,256,256]{2,1,0:T(8,128)(2,1)S(1)}, u32[]{:S(2)}, u32[]{:S(2)}) %collective-permute-start.29) | collective-permute-done | bytes 131104 | tf_op jit(solution)/shard_map/ppermute | solution.py:753
  200.8 6.6 %collective-permute-start.32 = (f32[64,128]{1,0:T(8,128)S(1)}, f32[64,128]{1,0:T(8,128)S(1)}, u32[]{:S(2)}, u32[]{:S(2)}) collective-permute-start(f32[64,128]{1,0:T(8,128)S(1)} %slice_select_fusion), channel_id=1, source_target_pairs={{0,8},{2,10},{4,12},{6,14},{8,0},{10,2},{12,4},{14,6},{1,9},{3,11}... | collective-permute-start | bytes 98312 | tf_op jit(solution)/shard_map/ppermute | solution.py:767
  207.4 1.9 collective-permute-done.32
  209.5 3.6 %collective-permute-done.33 = f32[32,128]{1,0:T(8,128)S(1)} collective-permute-done((f32[32,128]{1,0:T(8,128)S(1)}, f32[32,128]{1,0:T(8,128)S(1)}, u32[]{:S(2)}, u32[]{:S(2)}) %collective-permute-start.33) | collective-permute-done | bytes 16416 | tf_op jit(solution)/shard_map/ppermute | solution.py:767
  213.4 3.4 %collective-permute-done.34 = f32[16,128]{1,0:T(8,128)S(1)} collective-permute-done((f32[16,128]{1,0:T(8,128)S(1)}, f32[16,128]{1,0:T(8,128)S(1)}, u32[]{:S(2)}, u32[]{:S(2)}) %collective-permute-start.34) | collective-permute-done | bytes 8224 | tf_op jit(solution)/shard_map/ppermute | solution.py:767
  218.9 1.6 copy-done.6
  220.5 3.3 %finish.1 = f32[512,2048]{1,0:T(8,128)} custom-call(s32[48]{0:T(128)S(1)} %reshape.231.table_ref, s32[2]{0:T(128)S(1)} %copy-done.24, bf16[16,256,256]{2,1,0:T(8,128)(2,1)S(1)} %copy-done.6, bf16[16,256,256]{2,1,0:T(8,128)(2,1)S(1)} %copy-done.6, bf16[16,256,256]{2,1,0:T(8,128)(2,1)S(1)} %copy-done.6, bf16[16,256,256]{2,1,0:T(8,128)(2,1)S(1)} %copy-done.6, ...), custom_call_target="tpu_custom_call" | custom-call | flops 1000000 | bytes 100000 | tf_op jit(solution)/shard_map/finish/pallas_call | solution.py:570
  (171 shorter events, 35.0 us)
Async XLA Ops:
  0.6 17.1 %copy-start = (bf16[256,4096]{1,0:T(8,128)(2,1)S(1)}, bf16[256,4096]{1,0:T(8,128)(2,1)}, u32[]{:S(2)}) copy-start(bf16[256,4096]{1,0:T(8,128)(2,1)} %param.11) | copy-start | bytes 6291460
  4.8 19.1 %collective-permute-start.4 = (f32[64,512]{1,0:T(8,128)S(1)}, f32[64,512]{1,0:T(8,128)S(1)}, u32[]{:S(2)}, u32[]{:S(2)}) collective-permute-start(f32[64,512]{1,0:T(8,128)S(1)} %get-tuple-element.50), channel_id=1, source_target_pairs={{0,4},{2,6},{4,8},{6,10},{8,12},{10,14},{12,0},{14,2},{1,5},{3,7},... | collective-permute-start | bytes 393224 | tf_op jit(solution)/shard_map/ppermute | solution.py:598
  7.9 16.1 %collective-permute-start.5 = (f32[64,512]{1,0:T(8,128)S(1)}, f32[64,512]{1,0:T(8,128)S(1)}, u32[]{:S(2)}, u32[]{:S(2)}) collective-permute-start(f32[64,512]{1,0:T(8,128)S(1)} %get-tuple-element.52), channel_id=1, source_target_pairs={{0,8},{2,10},{4,12},{6,14},{8,0},{10,2},{12,4},{14,6},{1,9},{3,11}... | collective-permute-start | bytes 393224 | tf_op jit(solution)/shard_map/ppermute | solution.py:598
  10.5 7.3 %copy-start.27 = (bf16[4096,64]{0,1:T(8,128)(2,1)S(1)}, bf16[4096,64]{0,1:T(8,128)(2,1)}, u32[]{:S(2)}) copy-start(bf16[4096,64]{0,1:T(8,128)(2,1)} %param.13) | copy-start | bytes 1572868
  10.5 13.5 %collective-permute-start.6 = (f32[64,512]{1,0:T(8,128)S(1)}, f32[64,512]{1,0:T(8,128)S(1)}, u32[]{:S(2)}, u32[]{:S(2)}) collective-permute-start(f32[64,512]{1,0:T(8,128)S(1)} %get-tuple-element.51), channel_id=1, source_target_pairs={{0,12},{2,14},{4,0},{6,2},{8,4},{10,6},{12,8},{14,10},{1,13},{3,15... | collective-permute-start | bytes 393224 | tf_op jit(solution)/shard_map/ppermute | solution.py:598
  18.6 1.4 collective-permute-start
  21.6 14.8 %copy-start.25 = (bf16[16,4096]{1,0:T(8,128)(2,1)}, bf16[16,4096]{1,0:T(8,128)(2,1)S(1)}, u32[]{:S(2)}) copy-start(bf16[16,4096]{1,0:T(8,128)(2,1)S(1)} %convert_element_type.31.vectors_ref) | copy-start | bytes 393220
  21.7 5.0 %collective-permute-start.1 = (bf16[16,1024]{1,0:T(8,128)(2,1)S(1)}, bf16[16,1024]{1,0:T(8,128)(2,1)S(1)}, u32[]{:S(2)}, u32[]{:S(2)}) collective-permute-start(bf16[16,1024]{1,0:T(8,128)(2,1)S(1)} %get-tuple-element.69), channel_id=1, source_target_pairs={{0,12},{2,14},{4,0},{6,2},{8,4},{10,6},{12,8},{14,10},{1,13},{3,15... | collective-permute-start | bytes 98312 | tf_op jit(solution)/shard_map/ppermute | solution.py:598
  22.2 5.1 %collective-permute-start.2 = (bf16[16,1024]{1,0:T(8,128)(2,1)S(1)}, bf16[16,1024]{1,0:T(8,128)(2,1)S(1)}, u32[]{:S(2)}, u32[]{:S(2)}) collective-permute-start(bf16[16,1024]{1,0:T(8,128)(2,1)S(1)} %get-tuple-element.68), channel_id=1, source_target_pairs={{0,8},{2,10},{4,12},{6,14},{8,0},{10,2},{12,4},{14,6},{1,9},{3,11}... | collective-permute-start | bytes 98312 | tf_op jit(solution)/shard_map/ppermute | solution.py:598
  23.9 5.7 %collective-permute-start.3 = (bf16[16,1024]{1,0:T(8,128)(2,1)S(1)}, bf16[16,1024]{1,0:T(8,128)(2,1)S(1)}, u32[]{:S(2)}, u32[]{:S(2)}) collective-permute-start(bf16[16,1024]{1,0:T(8,128)(2,1)S(1)} %get-tuple-element.67), channel_id=1, source_target_pairs={{0,4},{2,6},{4,8},{6,10},{8,12},{10,14},{12,0},{14,2},{1,5},{3,7},... | collective-permute-start | bytes 98312 | tf_op jit(solution)/shard_map/ppermute | solution.py:598
  24.9 5.4 %collective-permute-start.7 = (f32[64,512]{1,0:T(8,128)S(1)}, f32[64,512]{1,0:T(8,128)S(1)}, u32[]{:S(2)}, u32[]{:S(2)}) collective-permute-start(f32[64,512]{1,0:T(8,128)S(1)} %add_add_fusion), channel_id=1, source_target_pairs={{0,2},{2,0},{4,6},{6,4},{8,10},{10,8},{12,14},{14,12},{1,3},{3,1},... | collective-permute-start | bytes 393224 | tf_op jit(solution)/shard_map/ppermute | solution.py:594
  30.4 6.0 %copy-start.26 = (f32[64,512]{1,0:T(8,128)}, f32[64,512]{1,0:T(8,128)S(1)}, u32[]{:S(2)}) copy-start(f32[64,512]{1,0:T(8,128)S(1)} %add.290.refs_1_) | copy-start | bytes 393220
  30.4 12.6 %collective-permute-start.10 = (f32[64,512]{1,0:T(8,128)S(1)}, f32[64,512]{1,0:T(8,128)S(1)}, u32[]{:S(2)}, u32[]{:S(2)}) collective-permute-start(f32[64,512]{1,0:T(8,128)S(1)} %add.290.refs_1_), channel_id=1, source_target_pairs={{0,4},{2,6},{4,8},{6,10},{8,12},{10,14},{12,0},{14,2},{1,5},{3,7},... | collective-permute-start | bytes 393224 | tf_op jit(solution)/shard_map/ppermute | solution.py:598
  31.7 11.3 %collective-permute-start.8 = (f32[64,512]{1,0:T(8,128)S(1)}, f32[64,512]{1,0:T(8,128)S(1)}, u32[]{:S(2)}, u32[]{:S(2)}) collective-permute-start(f32[64,512]{1,0:T(8,128)S(1)} %add.290.refs_1_), channel_id=1, source_target_pairs={{0,12},{2,14},{4,0},{6,2},{8,4},{10,6},{12,8},{14,10},{1,13},{3,15... | collective-permute-start | bytes 393224 | tf_op jit(solution)/shard_map/ppermute | solution.py:598
  34.2 10.2 %collective-permute-start.9 = (f32[64,512]{1,0:T(8,128)S(1)}, f32[64,512]{1,0:T(8,128)S(1)}, u32[]{:S(2)}, u32[]{:S(2)}) collective-permute-start(f32[64,512]{1,0:T(8,128)S(1)} %add.290.refs_1_), channel_id=1, source_target_pairs={{0,8},{2,10},{4,12},{6,14},{8,0},{10,2},{12,4},{14,6},{1,9},{3,11}... | collective-permute-start | bytes 393224 | tf_op jit(solution)/shard_map/ppermute | solution.py:598
  34.8 10.7 %collective-permute-start.11 = (bf16[64,768]{1,0:T(8,128)(2,1)S(1)}, bf16[64,768]{1,0:T(8,128)(2,1)S(1)}, u32[]{:S(2)}, u32[]{:S(2)}) collective-permute-start(bf16[64,768]{1,0:T(8,128)(2,1)S(1)} %broadcast_select_fusion.1.refs_0_), channel_id=1, source_target_pairs={{0,2},{2,0},{4,6},{6,4},{8,10},{10,8},{12,14},{14,12},{1,3},{3,1},... | collective-permute-start | bytes 294920 | tf_op jit(solution)/shard_map/ppermute | solution.py:594
  45.5 21.3 %copy-start.10 = (f32[256,512]{1,0:T(8,128)}, f32[256,512]{1,0:T(8,128)S(1)}, u32[]{:S(2)}) copy-start(f32[256,512]{1,0:T(8,128)S(1)} %pad_maximum_fusion.refs_2_.mine_ref) | copy-start | bytes 1572868
  45.5 14.7 %copy-start.17 = (bf16[64,768]{1,0:T(8,128)(2,1)}, bf16[64,768]{1,0:T(8,128)(2,1)S(1)}, u32[]{:S(2)}) copy-start(bf16[64,768]{1,0:T(8,128)(2,1)S(1)} %collective-permute-done.11.refs_3_.came_ref) | copy-start | bytes 294916
  45.6 19.0 %collective-permute-start.12 = (bf16[256,1280]{1,0:T(8,128)(2,1)S(1)}, bf16[256,1280]{1,0:T(8,128)(2,1)S(1)}, u32[]{:S(2)}, u32[]{:S(2)}) collective-permute-start(bf16[256,1280]{1,0:T(8,128)(2,1)S(1)} %get-tuple-element.28.refs_0_), channel_id=1, source_target_pairs={{0,4},{4,8},{8,12},{12,14},{14,10},{10,6},{6,2},{2,0},{1,5},{5,9},... | collective-permute-start | bytes 1966088 | tf_op jit(solution)/shard_map/ppermute | solution.py:713
  45.9 14.4 %collective-permute-start.15 = (bf16[256,1024]{1,0:T(8,128)(2,1)S(1)}, bf16[256,1024]{1,0:T(8,128)(2,1)S(1)}, u32[]{:S(2)}, u32[]{:S(2)}) collective-permute-start(bf16[256,1024]{1,0:T(8,128)(2,1)S(1)} %get-tuple-element.29), channel_id=1, source_target_pairs={{0,2},{4,0},{8,4},{12,8},{14,12},{10,14},{6,10},{2,6},{1,3},{5,1},... | collective-permute-start | bytes 1572872 | tf_op jit(solution)/shard_map/ppermute | solution.py:714
  63.0 31.7 %collective-permute-start.16 = (bf16[256,2304]{1,0:T(8,128)(2,1)S(1)}, bf16[256,2304]{1,0:T(8,128)(2,1)}, u32[]{:S(2)}, u32[]{:S(2)}) collective-permute-start(bf16[256,2304]{1,0:T(8,128)(2,1)S(1)} %add_terms.9.refs_1_), channel_id=1, source_target_pairs={{0,2},{4,0},{8,4},{12,8},{14,12},{10,14},{6,10},{2,6},{1,3},{5,1},... | collective-permute-start | bytes 3538952 | tf_op jit(solution)/shard_map/ppermute | solution.py:724
  66.0 33.0 %collective-permute-start.13 = (bf16[256,2304]{1,0:T(8,128)(2,1)}, bf16[256,2304]{1,0:T(8,128)(2,1)}, u32[]{:S(2)}, u32[]{:S(2)}) collective-permute-start(bf16[256,2304]{1,0:T(8,128)(2,1)} %add_terms.8.refs_0_), channel_id=1, source_target_pairs={{0,4},{4,8},{8,12},{12,14},{14,10},{10,6},{6,2},{2,0},{1,5},{5,9},... | collective-permute-start | bytes 3538952 | tf_op jit(solution)/shard_map/ppermute | solution.py:723
  66.8 1.9 collective-permute-start.14
  86.6 8.1 %slice-start = ((s8[4718592]{0:T(1024)(128)(4,1)}), s8[4194304]{0:T(1024)(128)(4,1)S(1)}, s32[]{:S(2)}) async-start(s8[4718592]{0:T(1024)(128)(4,1)} %bitcast.23), calls=%async_computation | async-start | bytes 8388608
  86.6 8.1 %slice-start.1 = ((s8[4718592]{0:T(1024)(128)(4,1)}), s8[524288]{0:T(1024)(128)(4,1)S(1)}, s32[]{:S(2)}) async-start(s8[4718592]{0:T(1024)(128)(4,1)} %bitcast.23), calls=%async_computation.1 | async-start | bytes 1048576
  97.4 43.7 %collective-permute-start.22 = (bf16[256,2304]{1,0:T(8,128)(2,1)S(1)}, bf16[256,2304]{1,0:T(8,128)(2,1)}, u32[]{:S(2)}, u32[]{:S(2)}) collective-permute-start(bf16[256,2304]{1,0:T(8,128)(2,1)S(1)} %add_terms.11.refs_1_), channel_id=1, source_target_pairs={{0,2},{4,0},{8,4},{12,8},{14,12},{10,14},{6,10},{2,6},{1,3},{5,1},... | collective-permute-start | bytes 3538952 | tf_op jit(solution)/shard_map/ppermute | solution.py:724
  101.8 45.6 %collective-permute-start.17 = (bf16[256,2304]{1,0:T(8,128)(2,1)}, bf16[256,2304]{1,0:T(8,128)(2,1)}, u32[]{:S(2)}, u32[]{:S(2)}) collective-permute-start(bf16[256,2304]{1,0:T(8,128)(2,1)} %add_terms.10.refs_0_), channel_id=1, source_target_pairs={{0,4},{4,8},{8,12},{12,14},{14,10},{10,6},{6,2},{2,0},{1,5},{5,9},... | collective-permute-start | bytes 3538952 | tf_op jit(solution)/shard_map/ppermute | solution.py:723
  102.4 29.5 %collective-permute-start.18 = (bf16[2,128,256]{2,1,0:T(8,128)(2,1)}, bf16[2,128,256]{2,1,0:T(8,128)(2,1)S(1)}, u32[]{:S(2)}, u32[]{:S(2)}) collective-permute-start(bf16[2,128,256]{2,1,0:T(8,128)(2,1)} %get-tuple-element.32), channel_id=1, source_target_pairs={{0,4},{2,6},{4,8},{6,10},{8,12},{10,14},{12,0},{14,2},{1,5},{3,7},... | collective-permute-start | bytes 393224 | tf_op jit(solution)/shard_map/ppermute | solution.py:598
  102.7 32.1 %collective-permute-start.19 = (bf16[2,128,256]{2,1,0:T(8,128)(2,1)}, bf16[2,128,256]{2,1,0:T(8,128)(2,1)S(1)}, u32[]{:S(2)}, u32[]{:S(2)}) collective-permute-start(bf16[2,128,256]{2,1,0:T(8,128)(2,1)} %get-tuple-element.33), channel_id=1, source_target_pairs={{0,8},{2,10},{4,12},{6,14},{8,0},{10,2},{12,4},{14,6},{1,9},{3,11}... | collective-permute-start | bytes 393224 | tf_op jit(solution)/shard_map/ppermute | solution.py:598
  105.2 31.2 %collective-permute-start.20 = (bf16[2,128,256]{2,1,0:T(8,128)(2,1)}, bf16[2,128,256]{2,1,0:T(8,128)(2,1)}, u32[]{:S(2)}, u32[]{:S(2)}) collective-permute-start(bf16[2,128,256]{2,1,0:T(8,128)(2,1)} %get-tuple-element.34), channel_id=1, source_target_pairs={{0,12},{2,14},{4,0},{6,2},{8,4},{10,6},{12,8},{14,10},{1,13},{3,15... | collective-permute-start | bytes 393224 | tf_op jit(solution)/shard_map/ppermute | solution.py:598
  106.5 29.9 %copy-start.15 = (bf16[2,128,256]{2,1,0:T(8,128)(2,1)S(1)}, bf16[2,128,256]{2,1,0:T(8,128)(2,1)}, u32[]{:S(2)}) copy-start(bf16[2,128,256]{2,1,0:T(8,128)(2,1)} %get-tuple-element.31.refs_1_.refs_0_) | copy-start | bytes 393220
  106.5 29.9 %copy-start.24 = (s32[2]{0:T(128)S(1)}, s32[2]{0:T(128)}, u32[]{:S(2)}) copy-start(s32[2]{0:T(128)} %pad_add_fusion.1.place_ref) | copy-start | bytes 28
  142.9 19.7 %collective-permute-start.23 = (bf16[256,1280]{1,0:T(8,128)(2,1)S(1)}, bf16[256,1280]{1,0:T(8,128)(2,1)}, u32[]{:S(2)}, u32[]{:S(2)}) collective-permute-start(bf16[256,1280]{1,0:T(8,128)(2,1)S(1)} %add_terms.13.refs_2_), channel_id=1, source_target_pairs={{0,2},{4,0},{8,4},{12,8},{14,12},{10,14},{6,10},{2,6},{1,3},{5,1},... | collective-permute-start | bytes 1966088 | tf_op jit(solution)/shard_map/ppermute | solution.py:742
  148.9 17.8 %collective-permute-start.21 = (bf16[256,1280]{1,0:T(8,128)(2,1)S(1)}, bf16[256,1280]{1,0:T(8,128)(2,1)}, u32[]{:S(2)}, u32[]{:S(2)}) collective-permute-start(bf16[256,1280]{1,0:T(8,128)(2,1)S(1)} %add_terms.12.refs_1_), channel_id=1, source_target_pairs={{0,4},{4,8},{8,12},{12,14},{14,10},{10,6},{6,2},{2,0},{1,5},{5,9},... | collective-permute-start | bytes 1966088 | tf_op jit(solution)/shard_map/ppermute | solution.py:742
  151.3 25.0 %collective-permute-start.25 = (bf16[256,1024]{1,0:T(8,128)(2,1)}, bf16[256,1024]{1,0:T(8,128)(2,1)}, u32[]{:S(2)}, u32[]{:S(2)}) collective-permute-start(bf16[256,1024]{1,0:T(8,128)(2,1)} %add_terms.15), channel_id=1, source_target_pairs={{0,2},{4,0},{8,4},{12,8},{14,12},{10,14},{6,10},{2,6},{1,3},{5,1},... | collective-permute-start | bytes 1572872 | tf_op jit(solution)/shard_map/ppermute | solution.py:743
  155.6 21.7 %collective-permute-start.24 = (bf16[256,1024]{1,0:T(8,128)(2,1)}, bf16[256,1024]{1,0:T(8,128)(2,1)}, u32[]{:S(2)}, u32[]{:S(2)}) collective-permute-start(bf16[256,1024]{1,0:T(8,128)(2,1)} %add_terms.14), channel_id=1, source_target_pairs={{0,4},{4,8},{8,12},{12,14},{14,10},{10,6},{6,2},{2,0},{1,5},{5,9},... | collective-permute-start | bytes 1572872 | tf_op jit(solution)/shard_map/ppermute | solution.py:743
  168.7 8.6 %copy-start.4 = (bf16[3,256,2304]{2,1,0:T(8,128)(2,1)S(1)}, bf16[3,256,2304]{2,1,0:T(8,128)(2,1)}, u32[]{:S(2)}) copy-start(bf16[3,256,2304]{2,1,0:T(8,128)(2,1)} %window_terms.5.refs_4_.terms_ref) | copy-start | bytes 10616836
  170.7 20.2 %collective-permute-start.26 = (bf16[2,256,256]{2,1,0:T(8,128)(2,1)S(1)}, bf16[2,256,256]{2,1,0:T(8,128)(2,1)S(1)}, u32[]{:S(2)}, u32[]{:S(2)}) collective-permute-start(bf16[2,256,256]{2,1,0:T(8,128)(2,1)S(1)} %get-tuple-element.38), channel_id=1, source_target_pairs={{0,12},{4,14},{8,10},{12,6},{14,2},{10,0},{6,4},{2,8},{1,13},{5,15... | collective-permute-start | bytes 786440 | tf_op jit(solution)/shard_map/ppermute | solution.py:753
  172.8 25.8 %collective-permute-start.31 = (bf16[128,256]{1,0:T(8,128)(2,1)S(1)}, bf16[128,256]{1,0:T(8,128)(2,1)S(1)}, u32[]{:S(2)}, u32[]{:S(2)}) collective-permute-start(bf16[128,256]{1,0:T(8,128)(2,1)S(1)} %get-tuple-element.35.refs_1_), channel_id=1, source_target_pairs={{0,2},{2,0},{4,6},{6,4},{8,10},{10,8},{12,14},{14,12},{1,3},{3,1},... | collective-permute-start | bytes 196616 | tf_op jit(solution)/shard_map/ppermute | solution.py:594
  173.0 19.9 %collective-permute-start.27 = (bf16[2,256,256]{2,1,0:T(8,128)(2,1)S(1)}, bf16[2,256,256]{2,1,0:T(8,128)(2,1)S(1)}, u32[]{:S(2)}, u32[]{:S(2)}) collective-permute-start(bf16[2,256,256]{2,1,0:T(8,128)(2,1)S(1)} %get-tuple-element.39), channel_id=1, source_target_pairs={{0,6},{4,2},{8,0},{12,4},{14,8},{10,12},{6,14},{2,10},{1,7},{5,3},... | collective-permute-start | bytes 786440 | tf_op jit(solution)/shard_map/ppermute | solution.py:753
  179.1 14.3 %collective-permute-start.28 = (bf16[2,256,256]{2,1,0:T(8,128)(2,1)S(1)}, bf16[2,256,256]{2,1,0:T(8,128)(2,1)S(1)}, u32[]{:S(2)}, u32[]{:S(2)}) collective-permute-start(bf16[2,256,256]{2,1,0:T(8,128)(2,1)S(1)} %get-tuple-element.40), channel_id=1, source_target_pairs={{0,2},{4,0},{8,4},{12,8},{14,12},{10,14},{6,10},{2,6},{1,3},{5,1},... | collective-permute-start | bytes 786440 | tf_op jit(solution)/shard_map/ppermute | solution.py:753
  189.6 7.7 %collective-permute-start.29 = (bf16[1,256,256]{2,1,0:T(8,128)(2,1)S(1)}, bf16[1,256,256]{2,1,0:T(8,128)(2,1)S(1)}, u32[]{:S(2)}, u32[]{:S(2)}) collective-permute-start(bf16[1,256,256]{2,1,0:T(8,128)(2,1)S(1)} %get-tuple-element.41), channel_id=1, source_target_pairs={{0,14},{4,10},{8,6},{12,2},{14,0},{10,4},{6,8},{2,12},{1,15},{5,11... | collective-permute-start | bytes 393224 | tf_op jit(solution)/shard_map/ppermute | solution.py:753
  198.6 19.4 %copy-start.31 = (s32[256]{0:T(256)S(1)}, s32[256]{0:T(256)}, u32[]{:S(2)}) copy-start(s32[256]{0:T(256)} %param.16) | copy-start | bytes 3076
  200.8 8.5 %collective-permute-start.32 = (f32[64,128]{1,0:T(8,128)S(1)}, f32[64,128]{1,0:T(8,128)S(1)}, u32[]{:S(2)}, u32[]{:S(2)}) collective-permute-start(f32[64,128]{1,0:T(8,128)S(1)} %slice_select_fusion), channel_id=1, source_target_pairs={{0,8},{2,10},{4,12},{6,14},{8,0},{10,2},{12,4},{14,6},{1,9},{3,11}... | collective-permute-start | bytes 98312 | tf_op jit(solution)/shard_map/ppermute | solution.py:767
  209.3 3.8 %collective-permute-start.33 = (f32[32,128]{1,0:T(8,128)S(1)}, f32[32,128]{1,0:T(8,128)S(1)}, u32[]{:S(2)}, u32[]{:S(2)}) collective-permute-start(f32[32,128]{1,0:T(8,128)S(1)} %slice_select_fusion.1), channel_id=1, source_target_pairs={{0,4},{2,6},{4,0},{6,2},{8,12},{10,14},{12,8},{14,10},{1,5},{3,7},... | collective-permute-start | bytes 49160 | tf_op jit(solution)/shard_map/ppermute | solution.py:767
  209.5 9.4 %collective-permute-start.30 = (bf16[8,256,256]{2,1,0:T(8,128)(2,1)}, bf16[8,256,256]{2,1,0:T(8,128)(2,1)S(1)}, u32[]{:S(2)}, u32[]{:S(2)}) collective-permute-start(bf16[8,256,256]{2,1,0:T(8,128)(2,1)} %copy-done.11), channel_id=1, source_target_pairs={{0,1},{1,0},{2,3},{3,2},{4,5},{5,4},{6,7},{7,6},{8,9},{9,8},{10,11... | collective-permute-start | bytes 3145736 | tf_op jit(solution)/shard_map/ppermute | solution.py:760
  213.1 3.7 %collective-permute-start.34 = (f32[16,128]{1,0:T(8,128)S(1)}, f32[16,128]{1,0:T(8,128)S(1)}, u32[]{:S(2)}, u32[]{:S(2)}) collective-permute-start(f32[16,128]{1,0:T(8,128)S(1)} %slice_select_fusion.2), channel_id=1, source_target_pairs={{0,2},{2,0},{4,6},{6,4},{8,10},{10,8},{12,14},{14,12},{1,3},{3,1},... | collective-permute-start | bytes 24584 | tf_op jit(solution)/shard_map/ppermute | solution.py:767
  216.8 1.2 collective-permute-start.35
  (24 other events, 47.2 us)

commit v2 on v1

--- a/solution.py
+++ b/solution.py
@@ -82,89 +82,118 @@
     blocks_in_all = sum(len(slots) for slots in parts)
     chunk = rows // 4
 
+    width = blocks_in_all * group
+    widths = [len(slots) * group for slots in parts]
+
     def kernel(place_ref, step_ref, stored_ref, vectors_ref, *refs):
-        outs, (held, total, arrived) = refs[len(after) : -3], refs[-3:]
+        outs, (held, total, made, arrived, left_for) = refs[len(after) : -5], refs[-5:]
         i = pl.program_id(0)
+        slot = lax.rem(i, 2)
         owner = lax.rem(ring.position_of(place_ref[0]) + step_ref[i] + ring.count, ring.count)
         core = place_ref[1]
 
         def load(index):
             rows_of = pl.ds(index * chunk, chunk)
             return pltpu.make_async_copy(stored_ref.at[rows_of], held.at[rows_of], arrived.at[index])
+
+        def leave(step):
+            copies, base = [], 0
+            for part, columns in enumerate(widths):
+                out_ref = outs[step * len(parts) + part]
+                source = made.at[step % 2, :, pl.ds(base, columns)]
+                copies.append(pltpu.make_async_copy(source, out_ref, left_for.at[step % 2, part]))
+                base += columns
+            return copies
 
         @pl.when(i == 0)
         def _():
             for index in range(4):
                 load(index).start()
 
+        for step in range(2, len(steps)):
+
+            @pl.when(i == step)
+            def _():
+                for copy in leave(step - 2):
+                    copy.wait()
+
         left = pl.ds(pl.multiple_of((2 * ring.index_at(owner) + core) * group, group), group)
         chips, base = [], 0
-        for part, slots in enumerate(parts):
+        for slots in parts:
             for offset, blocks, first in pairs_of(slots):
                 column = 2 * ring.index_at(owner + offset)
                 if blocks == 1:
                     column = column + jnp.where(owner < ring.half, core, 1 - core)
                 right = pl.ds(pl.multiple_of(column * group, blocks * group), blocks * group)
-                here = slice((base + first) * group, (base + first + blocks) * group)
-                chips.append((part, right, here, slice(first * group, (first + blocks) * group)))
+                chips.append((right, slice((base + first) * group, (base + first + blocks) * group)))
             base += len(slots)
         turned_new = vectors_ref[:, left].T
 
         @pl.when(i == 0)
         def _():
-            for _, right, here, _ in chips:
+            for right, here in chips:
                 total[:, here] = jnp.dot(turned_new, vectors_ref[:, right], preferred_element_type=jnp.float32)
             for index in range(4):
                 load(index).wait()
                 rows_of = slice(index * chunk, (index + 1) * chunk)
                 turned = held[rows_of, left].T
-                for part, right, here, there in chips:
+                for right, here in chips:
                     added = total[:, here] + jnp.dot(turned, held[rows_of, right], preferred_element_type=jnp.float32)
                     if index < 3:
                         total[:, here] = added
                     else:
-                        outs[part][0, :, there] = added.astype(jnp.bfloat16)
+                        made[0, :, here] = added.astype(jnp.bfloat16)
 
         if len(steps) > 1:
 
             @pl.when(i > 0)
             def _():
                 turned = held[:, left].T
-                for part, right, _, there in chips:
+                for right, here in chips:
                     added = jnp.dot(turned, held[:, right], preferred_element_type=jnp.float32)
                     added = added + jnp.dot(turned_new, vectors_ref[:, right], preferred_element_type=jnp.float32)
-                    outs[part][0, :, there] = added.astype(jnp.bfloat16)
-
-    def out(slots):
-        return pl.BlockSpec((1, group, len(slots) * group), lambda i, a, b: (i, 0, 0))
-
-    def shape(slots):
-        return jax.ShapeDtypeStruct((len(steps), group, len(slots) * group), jnp.bfloat16)
-
-    return pl.pallas_call(
+                    made[slot, :, here] = added.astype(jnp.bfloat16)
+
+        for step in range(len(steps)):
+
+            @pl.when(i == step)
+            def _():
+                for copy in leave(step):
+                    copy.start()
+
+        @pl.when(i == len(steps) - 1)
+        def _():
+            for step in range(max(len(steps) - 2, 0), len(steps)):
+                for copy in leave(step):
+                    copy.wait()
+
+    found = pl.pallas_call(
         kernel,
         grid_spec=pltpu.PrefetchScalarGridSpec(
             num_scalar_prefetch=2,
             grid=(len(steps),),
             in_specs=[MAIN, pl.BlockSpec((new_rows, full), lambda i, a, b: (0, 0))] + [ANYWHERE] * len(after),
-            out_specs=[out(slots) for slots in parts],
+            out_specs=[ANYWHERE] * (len(steps) * len(parts)),
             scratch_shapes=[
                 pltpu.VMEM((rows, full), jnp.bfloat16),
-                pltpu.VMEM((group, blocks_in_all * group), jnp.float32),
+                pltpu.VMEM((group, width), jnp.float32),
+                pltpu.VMEM((2, group, width), jnp.bfloat16),
                 pltpu.SemaphoreType.DMA((4,)),
+                pltpu.SemaphoreType.DMA((2, len(parts))),
             ],
         ),
-        out_shape=[shape(slots) for slots in parts],
+        out_shape=[jax.ShapeDtypeStruct((group, columns), jnp.bfloat16) for _ in steps for columns in widths],
         compiler_params=pltpu.CompilerParams(vmem_limit_bytes=VMEM_BYTES),
         cost_estimate=LIGHT,
         name="window_terms",
     )(place, taps, stored, vectors, *after)
-
-
-def add_terms(terms, index, arrived, base, count, group, after=()):
+    return [found[step * len(parts) : (step + 1) * len(parts)] for step in range(len(steps))]
+
+
+def add_terms(terms, arrived, base, count, group, after=()):
     def kernel(terms_ref, *refs):
         out_ref, own, done = refs[-3:]
-        fetch = pltpu.make_async_copy(terms_ref.at[index, :, pl.ds(base * group, count * group)], own, done)
+        fetch = pltpu.make_async_copy(terms_ref.at[:, pl.ds(base * group, count * group)], own, done)
         fetch.start()
         fetch.wait()
         for k in range(count):
@@ -207,16 +236,14 @@
 def close_window(terms, base, ahead, back, slots, group, after=()):
     count = len(slots)
     chips = [chip for chip in pairs_of(slots) if chip[0] != 0]
-    index = terms.shape[0] - 1
-
     def kernel(terms_ref, ahead_ref, back_ref, *refs):
         blocks_ref, turned_refs, (own, done) = refs[len(after)], refs[len(after) + 1 : -2], refs[-2:]
-        fetch = pltpu.make_async_copy(terms_ref.at[index], own, done)
+        fetch = pltpu.make_async_copy(terms_ref.at[:, pl.ds(base * group, count * group)], own, done)
         fetch.start()
         fetch.wait()
         for k in range(count):
             cols = slice(k * group, (k + 1) * group)
-            total = own[:, (base + k) * group : (base + k + 1) * group].astype(jnp.float32)
+            total = own[:, cols].astype(jnp.float32)
             total = total + ahead_ref[:, cols].astype(jnp.float32) + back_ref[:, cols].astype(jnp.float32)
             total = total.astype(jnp.bfloat16)
             blocks_ref[k] = total
@@ -230,7 +257,7 @@
         in_specs=[ANYWHERE, FAST, FAST] + [ANYWHERE] * len(after),
         out_specs=[FAST] * len(sizes),
         out_shape=[jax.ShapeDtypeStruct((size, group, group), jnp.bfloat16) for size in sizes],
-        scratch_shapes=[pltpu.VMEM(terms.shape[1:], jnp.bfloat16), pltpu.SemaphoreType.DMA],
+        scratch_shapes=[pltpu.VMEM((group, count * group), jnp.bfloat16), pltpu.SemaphoreType.DMA],
         compiler_params=pltpu.CompilerParams(vmem_limit_bytes=SMALL_BYTES),
         cost_estimate=LIGHT,
         name="close_window",
@@ -702,19 +729,18 @@
     corner_rows = [corner_second] + [far_shift(corner_second, step, owners) for step in range(1, pairs_count)]
     corner_rows = jnp.concatenate(natural(corner_rows, pair), axis=0)
     corner_other = lax.ppermute(corner_rows, "tensor", SWAP)
-    far, near = terms_of([half], [far_slots, near_slots], [away, corner_second])
-    far, near = far[0], near[0]
+    far, near = terms_of([half], [far_slots, near_slots], [away, corner_second])[0]
     second_steps = [half - 1, 1 - half, half - 2, 2 - half]
     far, near = gate([far, near], [corner_rows, received])
-    second = terms_of(second_steps, [slots], [far])[0]
+    second = terms_of(second_steps, [slots], [far])
     shape = (pairs_count, 1, examples, group)
     own_cols = in_order(side, kept[:, width:].reshape(shape), received[:, width:].reshape(shape), 1)
     own_cols = own_cols.reshape(all_examples, group).astype(jnp.float32)
     far_ahead = lax.ppermute(far, "dp", ahead)
     near_back = lax.ppermute(near, "dp", back)
     total = far_count + near_count
-    going = add_terms(second, 0, [(far_ahead, 0)], 0, total, group)
-    coming = add_terms(second, 1, [(near_back, far_count)], 0, total, group)
+    going = add_terms(second[0][0], [(far_ahead, 0)], 0, total, group)
+    coming = add_terms(second[1][0], [(near_back, far_count)], 0, total, group)
 
     solved, first_pairs = solve(place, pairs_count, corner_rows, corner_other, kept, received, [going, coming])
     pieces = spread_back(place, stored, solved, owners, group)
@@ -722,28 +748,31 @@
     for step in range(half - 2, 0, -1):
         came_ahead = lax.ppermute(going, "dp", ahead)
         came_back = lax.ppermute(coming, "dp", back)
-        own, index, token = (second, 2, [pieces[0]]) if step == half - 2 else (later, later_steps.index(step), [away])
+        if step == half - 2:
+            (own_ahead,), (own_back,) = second[2:]
+            token = [pieces[0]]
+        else:
+            index = later_steps.index(step)
+            (own_ahead,), (own_back,) = later[index : index + 2]
+            token = came[1:]
         if step == 1:
-            far_going = add_terms(own, index, [(came_ahead, 0)], 0, far_count, group, token)
-            far_coming = add_terms(own, index + 1, [(came_back, 0)], 0, far_count, group, token)
-            token = [far_going, far_coming]
-            near_going = add_terms(own, index, [(came_ahead, 0)], far_count, near_count, group, token)
-            near_coming = add_terms(own, index + 1, [(came_back, 0)], far_count, near_count, group, token)
-            token = [near_going, near_coming]
+            far_going = add_terms(own_ahead, [(came_ahead, 0)], 0, far_count, group, token)
+            far_coming = add_terms(own_back, [(came_back, 0)], 0, far_count, group, token)
+            terms, away = sum_pieces(place, came, [far_going, far_coming])
+            terms_other = pair_swap(away, owners)
+            near_going = add_terms(own_ahead, [(came_ahead, 0)], far_count, near_count, group, [away])
+            near_coming = add_terms(own_back, [(came_back, 0)], far_count, near_count, group, [away])
         else:
-            going = add_terms(own, index, [(came_ahead, 0)], 0, total, group, token)
-            coming = add_terms(own, index + 1, [(came_back, 0)], 0, total, group, token)
-            token = [going, coming]
+            going = add_terms(own_ahead, [(came_ahead, 0)], 0, total, group, token)
+            coming = add_terms(own_back, [(came_back, 0)], 0, total, group, token)
         if step == half - 2:
-            later = terms_of(later_steps, [slots], token)[0]
+            later = terms_of(later_steps, [slots], [going, coming])
             came = [pieces[0]] + [far_shift(pieces[index], index, owners) for index in range(1, pairs_count)]
-            terms, away = sum_pieces(place, came, [later])
-            terms_other = pair_swap(away, owners)
     far_sums = [lax.ppermute(far_going, "dp", ahead), lax.ppermute(far_coming, "dp", back)]
     near_sums = [lax.ppermute(near_going, "dp", ahead), lax.ppermute(near_coming, "dp", back)]
 
-    far = close_window(later, 0, *far_sums, far_slots, group)
-    near = close_window(later, far_count, *near_sums, near_slots, group, [far[0]])
+    far = close_window(later[-1][0], 0, *far_sums, far_slots, group)
+    near = close_window(later[-1][0], far_count, *near_sums, near_slots, group, [far[0]])
     turned = {}
     for (found, slots) in ((far, far_slots), (near, near_slots)):
         chips = [chip for chip in pairs_of(slots) if chip[0] != 0]
@@ -759,7 +788,7 @@
     send = for_sibling(send_table, blocks, group)
     other = lax.ppermute(send, "tensor", SWAP)
 
-    pairs = pair_products(place, own_cols, first_pairs, terms, terms_other, solved, [send])
+    pairs = pair_products(place, own_cols, first_pairs, terms, terms_other, solved, [shifted[ring.offsets[0]]])
     bit = owners // 2
     while bit >= 1:
         kept_rows = jnp.where((d & bit) == 0, pairs[: pairs.shape[0] // 2], pairs[pairs.shape[0] // 2 :])

time: 226 us -> 258 us (1.14); the launches traced: 224 us -> 259 us
  Pallas kernels: 79 us -> 121 us
  starting transfers between devices: 58.5 us -> 53.6 us
  local copies, waits for them, and re-layouts: 18.2 us -> 15.1 us
    pallas_call x1, Pallas kernels: 17.1 us -> 62.5 us  [solve(): pl.pallas_call(kernel, in_specs=[pl.BlockSpec(memory_space=pltpu.SMEM)] +...]
    ppermute x3, starting transfers between devices: 6.83 us -> 0.21 us  [local(): lax.ppermute(sent_rows, 'dp', [(index, index ^ bit) for index in range(ow...]
    ppermute x4, waiting for transfers between devices: 6.34 us -> 0.65 us  [local(): lax.ppermute(turned[offset], 'dp', ring.shift(offset))]
    ppermute x3, waiting for transfers between devices: 8.88 us -> 13.1 us  [local(): lax.ppermute(sent_rows, 'dp', [(index, index ^ bit) for index in range(ow...]
    unnamed x73 -> x83, local copies, waits for them, and re-layouts: 13.9 us -> 10.8 us
  transfers between devices with their start and end apart: 36 -> 36, of which waited for: 19 -> 16; matrix products, arithmetic and copies ran while one was open for 6% -> 6% of each run, Pallas kernels for 33% -> 46%
where the time goes in v2:
time: 258 us; the launch traced here: 259 us
  Pallas kernels  121 us (47%)
  starting transfers between devices  53.6 us (21%)
  waiting for transfers between devices  52.7 us (20%)
  local copies, waits for them, and re-layouts  15.1 us (6%)
  matrix products  9.91 us (4%)
  other arithmetic  4.89 us (2%)
    pallas_call x1, Pallas kernels, solve(): pl.pallas_call(kernel, in_specs=[pl.BlockSpec(memory_space=pltpu.SMEM)] +...  62.5 us
    pallas_call x3, Pallas kernels, window_terms(): pl.pallas_call(kernel, grid_spec=pltpu.PrefetchScalarGridSpec(num_scalar_...  29.8 us
    ppermute x12, waiting for transfers between devices, far_shift(): lax.ppermute(value, 'dp', [(index, (index + 2 * step) % count) for index...  22 us
    ppermute x4, starting transfers between devices, local(): lax.ppermute(turned[offset], 'dp', ring.shift(offset))  18.5 us
    ppermute x12, starting transfers between devices, far_shift(): lax.ppermute(value, 'dp', [(index, (index + 2 * step) % count) for index...  18.2 us
    ppermute x3, waiting for transfers between devices, local(): lax.ppermute(sent_rows, 'dp', [(index, index ^ bit) for index in range(ow...  13.1 us
    pallas_call x8, Pallas kernels, add_terms(): pl.pallas_call(kernel, in_specs=[ANYWHERE] + [FAST] * len(arrived) + [ANY...  11.8 us
    unnamed x83, local copies, waits for them, and re-layouts  10.8 us
  transfers between devices with their start and end apart: 36, of which 16 were waited for; matrix products, arithmetic and copies ran while one was open for 6% of the time, Pallas kernels for 46%

profile of v2, /device:TPU:0, one launch (start us, length us, event | category | flops | bytes accessed | tf_op | source)
XLA Modules:
  0.0 258.8 jit_solution(10372158026449349184)
XLA Ops:
  0.7 1.8 slice-done.1
  4.8 3.1 %collective-permute-start.4 = (f32[64,512]{1,0:T(8,128)S(1)}, f32[64,512]{1,0:T(8,128)S(1)}, u32[]{:S(2)}, u32[]{:S(2)}) collective-permute-start(f32[64,512]{1,0:T(8,128)S(1)} %get-tuple-element.64), channel_id=1, source_target_pairs={{0,4},{2,6},{4,8},{6,10},{8,12},{10,14},{12,0},{14,2},{1,5},{3,7},... | collective-permute-start | bytes 393224 | tf_op jit(solution)/shard_map/ppermute | solution.py:625
  7.9 2.6 %collective-permute-start.5 = (f32[64,512]{1,0:T(8,128)S(1)}, f32[64,512]{1,0:T(8,128)S(1)}, u32[]{:S(2)}, u32[]{:S(2)}) collective-permute-start(f32[64,512]{1,0:T(8,128)S(1)} %get-tuple-element.66), channel_id=1, source_target_pairs={{0,8},{2,10},{4,12},{6,14},{8,0},{10,2},{12,4},{14,6},{1,9},{3,11}... | collective-permute-start | bytes 393224 | tf_op jit(solution)/shard_map/ppermute | solution.py:625
  10.5 1.3 collective-permute-start.6
  11.8 5.9 %fusion.29 = f32[256,64]{0,1:T(8,128)S(1)} fusion(bf16[256,14336]{1,0:T(8,128)(2,1)} %param.10, bf16[14336,64]{0,1:T(8,128)(2,1)} %param.12), kind=kOutput, calls=%fused_computation.118 | convolution fusion | flops 469762048 | bytes 9240576 | tf_op jit(solution)/shard_map/dot_general | solution.py:677
  22.2 1.7 collective-permute-start.2
  24.9 1.7 collective-permute-start.7
  27.2 2.3 collective-permute-done.3
  30.4 1.3 collective-permute-start.10
  31.7 2.5 collective-permute-start.8
  34.8 1.6 collective-permute-start.11
  36.4 6.7 %window_terms.3 = (bf16[256,1280]{1,0:T(8,128)(2,1)}, bf16[256,1024]{1,0:T(8,128)(2,1)}) custom-call(s32[2]{0:T(128)} %pad_add_fusion.1.place_ref, s32[1]{0:T(128)} %constant.135.clone.step_ref, bf16[1024,4096]{1,0:T(8,128)(2,1)} %stored_ref.5, bf16[16,4096]{1,0:T(8,128)(2,1)} %copy-done.30, bf16[64,768]{1,0:T(8,128)(2,1)} %copy-done.34, f32[64,512]{1,0:T(8,128)} %copy-done.31), custom_call_target="tpu_custom_call" | custom-call | flops 1000000 | bytes 100000 | tf_op jit(solution)/shard_map/window_terms/pallas_call | solution.py:170
  43.2 1.3 collective-permute-done.9
  46.0 1.6 collective-permute-start.15
  47.6 12.5 %window_terms.4 = (bf16[256,2304]{1,0:T(8,128)(2,1)}, bf16[256,2304]{1,0:T(8,128)(2,1)}, bf16[256,2304]{1,0:T(8,128)(2,1)}, bf16[256,2304]{1,0:T(8,128)(2,1)}) custom-call(s32[2]{0:T(128)} %pad_add_fusion.1.place_ref, s32[4]{0:T(128)} %constant.136.clone.step_ref, bf16[1024,4096]{1,0:T(8,128)(2,1)} %stored_ref.5, bf16[16,4096]{1,0:T(8,128)(2,1)} %copy-done.30, ...), custom_call_target="tpu_custom_call" | custom-call | flops 1000000 | bytes 100000 | tf_op jit(solution)/shard_map/window_terms/pallas_call | solution.py:170
  61.9 1.6 collective-permute-start.16
  64.6 1.9 collective-permute-done.14.other_ref
  67.4 62.5 %solve.1 = (f32[512,128]{1,0:T(8,128)}, f32[128,128]{1,0:T(8,128)}) custom-call(s32[2]{0:T(128)} %pad_add_fusion.1.place_ref, f32[256,512]{1,0:T(8,128)} %copy-done.11, f32[256,512]{1,0:T(8,128)} %copy-done.33, bf16[64,768]{1,0:T(8,128)(2,1)} %get-tuple-element.58.kept_ref, bf16[64,768]{1,0:T(8,128)(2,1)} %copy-done.26, bf16[256,2304]{1,0:T(8,128)(2,1)} %copy-done.10, ...), custom_call_target="tpu_custom_call" | custom-call | flops 1000000 | bytes 100000 | tf_op jit(solution)/shard_map/solve/pallas_call | solution.py:385
  129.9 7.7 %spread_back.1 = (bf16[2,128,256]{2,1,0:T(8,128)(2,1)}, bf16[2,128,256]{2,1,0:T(8,128)(2,1)}, bf16[2,128,256]{2,1,0:T(8,128)(2,1)}, bf16[2,128,256]{2,1,0:T(8,128)(2,1)}) custom-call(s32[2]{0:T(128)} %pad_add_fusion.1.place_ref, bf16[1024,4096]{1,0:T(8,128)(2,1)} %stored_ref.5, f32[512,128]{1,0:T(8,128)} %get-tuple-element.40.solved_ref, ...), custom_call_target="tpu_custom_call" | custom-call | flops 1000000 | bytes 100000 | tf_op jit(solution)/shard_map/spread_back/pallas_call | solution.py:423
  141.3 1.6 collective-permute-start.22
  142.9 2.8 %add_terms.10.refs_0_ = bf16[256,2304]{1,0:T(8,128)(2,1)} custom-call(bf16[256,2304]{1,0:T(8,128)(2,1)S(1)} %copy-done.14, bf16[256,2304]{1,0:T(8,128)(2,1)} %collective-permute-done.13.refs_0_, bf16[2,128,256]{2,1,0:T(8,128)(2,1)S(1)} %copy-done.19), custom_call_target="tpu_custom_call" | custom-call | flops 1000000 | bytes 100000 | tf_op jit(solution)/shard_map/add_terms/pallas_call | solution.py:208
  147.3 2.5 collective-permute-start.19
  149.9 1.4 collective-permute-start.20
  151.9 10.6 %window_terms.5 = (bf16[256,2304]{1,0:T(8,128)(2,1)}, bf16[256,2304]{1,0:T(8,128)(2,1)}, bf16[256,2304]{1,0:T(8,128)(2,1)}) custom-call(s32[2]{0:T(128)} %pad_add_fusion.1.place_ref, s32[3]{0:T(128)} %constant.137.clone.step_ref, bf16[1024,4096]{1,0:T(8,128)(2,1)} %stored_ref.5, bf16[16,4096]{1,0:T(8,128)(2,1)} %copy-done.30, ...), custom_call_target="tpu_custom_call" | custom-call | flops 1000000 | bytes 100000 | tf_op jit(solution)/shard_map/window_terms/pallas_call | solution.py:170
  162.5 13.2 %collective-permute-done.18.refs_1_ = bf16[2,128,256]{2,1,0:T(8,128)(2,1)S(1)} collective-permute-done((bf16[2,128,256]{2,1,0:T(8,128)(2,1)}, bf16[2,128,256]{2,1,0:T(8,128)(2,1)S(1)}, u32[]{:S(2)}, u32[]{:S(2)}) %collective-permute-start.18) | collective-permute-done | bytes 131104 | tf_op jit(solution)/shard_map/ppermute | solution.py:625
  175.7 2.9 %collective-permute-done.19.refs_2_ = bf16[2,128,256]{2,1,0:T(8,128)(2,1)S(1)} collective-permute-done((bf16[2,128,256]{2,1,0:T(8,128)(2,1)}, bf16[2,128,256]{2,1,0:T(8,128)(2,1)S(1)}, u32[]{:S(2)}, u32[]{:S(2)}) %collective-permute-start.19) | collective-permute-done | bytes 131104 | tf_op jit(solution)/shard_map/ppermute | solution.py:625
  178.6 1.7 collective-permute-done.20.refs_3_
  180.3 1.3 copy-done.7
  181.5 2.4 add_terms.13.refs_5_
  184.6 3.8 %collective-permute-start.23 = (bf16[256,1280]{1,0:T(8,128)(2,1)}, bf16[256,1280]{1,0:T(8,128)(2,1)}, u32[]{:S(2)}, u32[]{:S(2)}) collective-permute-start(bf16[256,1280]{1,0:T(8,128)(2,1)} %add_terms.13.refs_5_), channel_id=1, source_target_pairs={{0,2},{4,0},{8,4},{12,8},{14,12},{10,14},{6,10},{2,6},{1,3},{5,1},... | collective-permute-start | bytes 1966088 | tf_op jit(solution)/shard_map/ppermute | solution.py:771
  189.3 2.4 add_terms.12.refs_4_
  194.0 1.4 add_terms.15
  195.5 2.6 %collective-permute-start.25 = (bf16[256,1024]{1,0:T(8,128)(2,1)S(1)}, bf16[256,1024]{1,0:T(8,128)(2,1)S(1)}, u32[]{:S(2)}, u32[]{:S(2)}) collective-permute-start(bf16[256,1024]{1,0:T(8,128)(2,1)S(1)} %add_terms.15), channel_id=1, source_target_pairs={{0,2},{4,0},{8,4},{12,8},{14,12},{10,14},{6,10},{2,6},{1,3},{5,1},... | collective-permute-start | bytes 1572872 | tf_op jit(solution)/shard_map/ppermute | solution.py:772
  198.2 1.4 add_terms.14
  200.5 3.5 %collective-permute-done.23.back_ref = bf16[256,1280]{1,0:T(8,128)(2,1)} collective-permute-done((bf16[256,1280]{1,0:T(8,128)(2,1)}, bf16[256,1280]{1,0:T(8,128)(2,1)}, u32[]{:S(2)}, u32[]{:S(2)}) %collective-permute-start.23) | collective-permute-done | bytes 655392 | tf_op jit(solution)/shard_map/ppermute | solution.py:771
  204.1 6.3 %collective-permute-done.21.ahead_ref = bf16[256,1280]{1,0:T(8,128)(2,1)} collective-permute-done((bf16[256,1280]{1,0:T(8,128)(2,1)}, bf16[256,1280]{1,0:T(8,128)(2,1)}, u32[]{:S(2)}, u32[]{:S(2)}) %collective-permute-start.21) | collective-permute-done | bytes 655392 | tf_op jit(solution)/shard_map/ppermute | solution.py:771
  210.3 1.7 close_window.2
  212.0 2.0 collective-permute-start.26
  214.2 3.3 %collective-permute-start.27 = (bf16[2,256,256]{2,1,0:T(8,128)(2,1)S(1)}, bf16[2,256,256]{2,1,0:T(8,128)(2,1)S(1)}, u32[]{:S(2)}, u32[]{:S(2)}) collective-permute-start(bf16[2,256,256]{2,1,0:T(8,128)(2,1)S(1)} %get-tuple-element.53), channel_id=1, source_target_pairs={{0,6},{4,2},{8,0},{12,4},{14,8},{10,12},{6,14},{2,10},{1,7},{5,3},... | collective-permute-start | bytes 786440 | tf_op jit(solution)/shard_map/ppermute | solution.py:782
  217.5 3.5 %collective-permute-done.24.ahead_ref = bf16[256,1024]{1,0:T(8,128)(2,1)S(1)} collective-permute-done((bf16[256,1024]{1,0:T(8,128)(2,1)S(1)}, bf16[256,1024]{1,0:T(8,128)(2,1)S(1)}, u32[]{:S(2)}, u32[]{:S(2)}) %collective-permute-start.24) | collective-permute-done | bytes 524320 | tf_op jit(solution)/shard_map/ppermute | solution.py:772
  221.4 10.3 %collective-permute-start.28 = (bf16[2,256,256]{2,1,0:T(8,128)(2,1)S(1)}, bf16[2,256,256]{2,1,0:T(8,128)(2,1)S(1)}, u32[]{:S(2)}, u32[]{:S(2)}) collective-permute-start(bf16[2,256,256]{2,1,0:T(8,128)(2,1)S(1)} %get-tuple-element.54), channel_id=1, source_target_pairs={{0,2},{4,0},{8,4},{12,8},{14,12},{10,14},{6,10},{2,6},{1,3},{5,1},... | collective-permute-start | bytes 786440 | tf_op jit(solution)/shard_map/ppermute | solution.py:782
  231.6 3.0 %collective-permute-start.29 = (bf16[1,256,256]{2,1,0:T(8,128)(2,1)S(1)}, bf16[1,256,256]{2,1,0:T(8,128)(2,1)S(1)}, u32[]{:S(2)}, u32[]{:S(2)}) collective-permute-start(bf16[1,256,256]{2,1,0:T(8,128)(2,1)S(1)} %get-tuple-element.55), channel_id=1, source_target_pairs={{0,14},{4,10},{8,6},{12,2},{14,0},{10,4},{6,8},{2,12},{1,15},{5,11... | collective-permute-start | bytes 393224 | tf_op jit(solution)/shard_map/ppermute | solution.py:782
  236.8 7.5 %collective-permute-done.32 = f32[64,128]{1,0:T(8,128)S(1)} collective-permute-done((f32[64,128]{1,0:T(8,128)S(1)}, f32[64,128]{1,0:T(8,128)S(1)}, u32[]{:S(2)}, u32[]{:S(2)}) %collective-permute-start.32) | collective-permute-done | bytes 32800 | tf_op jit(solution)/shard_map/ppermute | solution.py:796
  244.5 1.6 for_sibling.1
  246.1 2.0 collective-permute-done.33
  248.3 3.6 %collective-permute-done.34 = f32[16,128]{1,0:T(8,128)S(1)} collective-permute-done((f32[16,128]{1,0:T(8,128)S(1)}, f32[16,128]{1,0:T(8,128)S(1)}, u32[]{:S(2)}, u32[]{:S(2)}) %collective-permute-start.34) | collective-permute-done | bytes 8224 | tf_op jit(solution)/shard_map/ppermute | solution.py:796
  253.9 1.6 copy-done.2
  255.5 3.3 %finish.1 = f32[512,2048]{1,0:T(8,128)} custom-call(s32[48]{0:T(128)S(1)} %reshape.231.table_ref, s32[2]{0:T(128)S(1)} %copy-done.29, bf16[16,256,256]{2,1,0:T(8,128)(2,1)S(1)} %copy-done.2, bf16[16,256,256]{2,1,0:T(8,128)(2,1)S(1)} %copy-done.2, bf16[16,256,256]{2,1,0:T(8,128)(2,1)S(1)} %copy-done.2, bf16[16,256,256]{2,1,0:T(8,128)(2,1)S(1)} %copy-done.2, ...), custom_call_target="tpu_custom_call" | custom-call | flops 1000000 | bytes 100000 | tf_op jit(solution)/shard_map/finish/pallas_call | solution.py:597
  (180 shorter events, 30.4 us)
Async XLA Ops:
  0.6 17.1 %copy-start = (bf16[256,4096]{1,0:T(8,128)(2,1)S(1)}, bf16[256,4096]{1,0:T(8,128)(2,1)}, u32[]{:S(2)}) copy-start(bf16[256,4096]{1,0:T(8,128)(2,1)} %param.11) | copy-start | bytes 6291460
  4.8 19.1 %collective-permute-start.4 = (f32[64,512]{1,0:T(8,128)S(1)}, f32[64,512]{1,0:T(8,128)S(1)}, u32[]{:S(2)}, u32[]{:S(2)}) collective-permute-start(f32[64,512]{1,0:T(8,128)S(1)} %get-tuple-element.64), channel_id=1, source_target_pairs={{0,4},{2,6},{4,8},{6,10},{8,12},{10,14},{12,0},{14,2},{1,5},{3,7},... | collective-permute-start | bytes 393224 | tf_op jit(solution)/shard_map/ppermute | solution.py:625
  7.9 16.1 %collective-permute-start.5 = (f32[64,512]{1,0:T(8,128)S(1)}, f32[64,512]{1,0:T(8,128)S(1)}, u32[]{:S(2)}, u32[]{:S(2)}) collective-permute-start(f32[64,512]{1,0:T(8,128)S(1)} %get-tuple-element.66), channel_id=1, source_target_pairs={{0,8},{2,10},{4,12},{6,14},{8,0},{10,2},{12,4},{14,6},{1,9},{3,11}... | collective-permute-start | bytes 393224 | tf_op jit(solution)/shard_map/ppermute | solution.py:625
  10.5 13.5 %collective-permute-start.6 = (f32[64,512]{1,0:T(8,128)S(1)}, f32[64,512]{1,0:T(8,128)S(1)}, u32[]{:S(2)}, u32[]{:S(2)}) collective-permute-start(f32[64,512]{1,0:T(8,128)S(1)} %get-tuple-element.65), channel_id=1, source_target_pairs={{0,12},{2,14},{4,0},{6,2},{8,4},{10,6},{12,8},{14,10},{1,13},{3,15... | collective-permute-start | bytes 393224 | tf_op jit(solution)/shard_map/ppermute | solution.py:625
  18.6 1.4 collective-permute-start
  21.6 14.8 %copy-start.30 = (bf16[16,4096]{1,0:T(8,128)(2,1)}, bf16[16,4096]{1,0:T(8,128)(2,1)S(1)}, u32[]{:S(2)}) copy-start(bf16[16,4096]{1,0:T(8,128)(2,1)S(1)} %convert_element_type.31.vectors_ref) | copy-start | bytes 393220
  21.7 5.0 %collective-permute-start.1 = (bf16[16,1024]{1,0:T(8,128)(2,1)S(1)}, bf16[16,1024]{1,0:T(8,128)(2,1)S(1)}, u32[]{:S(2)}, u32[]{:S(2)}) collective-permute-start(bf16[16,1024]{1,0:T(8,128)(2,1)S(1)} %get-tuple-element.83), channel_id=1, source_target_pairs={{0,12},{2,14},{4,0},{6,2},{8,4},{10,6},{12,8},{14,10},{1,13},{3,15... | collective-permute-start | bytes 98312 | tf_op jit(solution)/shard_map/ppermute | solution.py:625
  22.2 5.1 %collective-permute-start.2 = (bf16[16,1024]{1,0:T(8,128)(2,1)S(1)}, bf16[16,1024]{1,0:T(8,128)(2,1)S(1)}, u32[]{:S(2)}, u32[]{:S(2)}) collective-permute-start(bf16[16,1024]{1,0:T(8,128)(2,1)S(1)} %get-tuple-element.82), channel_id=1, source_target_pairs={{0,8},{2,10},{4,12},{6,14},{8,0},{10,2},{12,4},{14,6},{1,9},{3,11}... | collective-permute-start | bytes 98312 | tf_op jit(solution)/shard_map/ppermute | solution.py:625
  23.9 5.7 %collective-permute-start.3 = (bf16[16,1024]{1,0:T(8,128)(2,1)S(1)}, bf16[16,1024]{1,0:T(8,128)(2,1)S(1)}, u32[]{:S(2)}, u32[]{:S(2)}) collective-permute-start(bf16[16,1024]{1,0:T(8,128)(2,1)S(1)} %get-tuple-element.81), channel_id=1, source_target_pairs={{0,4},{2,6},{4,8},{6,10},{8,12},{10,14},{12,0},{14,2},{1,5},{3,7},... | collective-permute-start | bytes 98312 | tf_op jit(solution)/shard_map/ppermute | solution.py:625
  24.9 5.5 %collective-permute-start.7 = (f32[64,512]{1,0:T(8,128)S(1)}, f32[64,512]{1,0:T(8,128)S(1)}, u32[]{:S(2)}, u32[]{:S(2)}) collective-permute-start(f32[64,512]{1,0:T(8,128)S(1)} %add_add_fusion), channel_id=1, source_target_pairs={{0,2},{2,0},{4,6},{6,4},{8,10},{10,8},{12,14},{14,12},{1,3},{3,1},... | collective-permute-start | bytes 393224 | tf_op jit(solution)/shard_map/ppermute | solution.py:621
  30.4 12.8 %collective-permute-start.10 = (f32[64,512]{1,0:T(8,128)S(1)}, f32[64,512]{1,0:T(8,128)S(1)}, u32[]{:S(2)}, u32[]{:S(2)}) collective-permute-start(f32[64,512]{1,0:T(8,128)S(1)} %add.290.refs_1_), channel_id=1, source_target_pairs={{0,4},{2,6},{4,8},{6,10},{8,12},{10,14},{12,0},{14,2},{1,5},{3,7},... | collective-permute-start | bytes 393224 | tf_op jit(solution)/shard_map/ppermute | solution.py:625
  31.7 11.4 %collective-permute-start.8 = (f32[64,512]{1,0:T(8,128)S(1)}, f32[64,512]{1,0:T(8,128)S(1)}, u32[]{:S(2)}, u32[]{:S(2)}) collective-permute-start(f32[64,512]{1,0:T(8,128)S(1)} %add.290.refs_1_), channel_id=1, source_target_pairs={{0,12},{2,14},{4,0},{6,2},{8,4},{10,6},{12,8},{14,10},{1,13},{3,15... | collective-permute-start | bytes 393224 | tf_op jit(solution)/shard_map/ppermute | solution.py:625
  34.3 10.2 %collective-permute-start.9 = (f32[64,512]{1,0:T(8,128)S(1)}, f32[64,512]{1,0:T(8,128)S(1)}, u32[]{:S(2)}, u32[]{:S(2)}) collective-permute-start(f32[64,512]{1,0:T(8,128)S(1)} %add.290.refs_1_), channel_id=1, source_target_pairs={{0,8},{2,10},{4,12},{6,14},{8,0},{10,2},{12,4},{14,6},{1,9},{3,11}... | collective-permute-start | bytes 393224 | tf_op jit(solution)/shard_map/ppermute | solution.py:625
  34.8 10.7 %collective-permute-start.11 = (bf16[64,768]{1,0:T(8,128)(2,1)S(1)}, bf16[64,768]{1,0:T(8,128)(2,1)S(1)}, u32[]{:S(2)}, u32[]{:S(2)}) collective-permute-start(bf16[64,768]{1,0:T(8,128)(2,1)S(1)} %broadcast_select_fusion.1.refs_0_), channel_id=1, source_target_pairs={{0,2},{2,0},{4,6},{6,4},{8,10},{10,8},{12,14},{14,12},{1,3},{3,1},... | collective-permute-start | bytes 294920 | tf_op jit(solution)/shard_map/ppermute | solution.py:621
  45.5 19.2 %copy-start.11 = (f32[256,512]{1,0:T(8,128)}, f32[256,512]{1,0:T(8,128)S(1)}, u32[]{:S(2)}) copy-start(f32[256,512]{1,0:T(8,128)S(1)} %pad_maximum_fusion.refs_2_.mine_ref) | copy-start | bytes 1572868
  45.5 14.7 %copy-start.26 = (bf16[64,768]{1,0:T(8,128)(2,1)}, bf16[64,768]{1,0:T(8,128)(2,1)S(1)}, u32[]{:S(2)}) copy-start(bf16[64,768]{1,0:T(8,128)(2,1)S(1)} %collective-permute-done.11.refs_3_.came_ref) | copy-start | bytes 294916
  45.6 17.9 %collective-permute-start.12 = (bf16[256,1280]{1,0:T(8,128)(2,1)S(1)}, bf16[256,1280]{1,0:T(8,128)(2,1)S(1)}, u32[]{:S(2)}, u32[]{:S(2)}) collective-permute-start(bf16[256,1280]{1,0:T(8,128)(2,1)S(1)} %get-tuple-element.35.refs_0_), channel_id=1, source_target_pairs={{0,4},{4,8},{8,12},{12,14},{14,10},{10,6},{6,2},{2,0},{1,5},{5,9},... | collective-permute-start | bytes 1966088 | tf_op jit(solution)/shard_map/ppermute | solution.py:739
  46.0 14.2 %collective-permute-start.15 = (bf16[256,1024]{1,0:T(8,128)(2,1)S(1)}, bf16[256,1024]{1,0:T(8,128)(2,1)S(1)}, u32[]{:S(2)}, u32[]{:S(2)}) collective-permute-start(bf16[256,1024]{1,0:T(8,128)(2,1)S(1)} %get-tuple-element.39), channel_id=1, source_target_pairs={{0,2},{4,0},{8,4},{12,8},{14,12},{10,14},{6,10},{2,6},{1,3},{5,1},... | collective-permute-start | bytes 1572872 | tf_op jit(solution)/shard_map/ppermute | solution.py:740
  61.9 75.7 %collective-permute-start.16 = (bf16[256,2304]{1,0:T(8,128)(2,1)S(1)}, bf16[256,2304]{1,0:T(8,128)(2,1)S(1)}, u32[]{:S(2)}, u32[]{:S(2)}) collective-permute-start(bf16[256,2304]{1,0:T(8,128)(2,1)S(1)} %add_terms.9.refs_1_), channel_id=1, source_target_pairs={{0,2},{4,0},{8,4},{12,8},{14,12},{10,14},{6,10},{2,6},{1,3},{5,1},... | collective-permute-start | bytes 3538952 | tf_op jit(solution)/shard_map/ppermute | solution.py:750
  63.9 79.0 %collective-permute-start.13 = (bf16[256,2304]{1,0:T(8,128)(2,1)S(1)}, bf16[256,2304]{1,0:T(8,128)(2,1)}, u32[]{:S(2)}, u32[]{:S(2)}) collective-permute-start(bf16[256,2304]{1,0:T(8,128)(2,1)S(1)} %add_terms.8.refs_0_), channel_id=1, source_target_pairs={{0,4},{4,8},{8,12},{12,14},{14,10},{10,6},{6,2},{2,0},{1,5},{5,9},... | collective-permute-start | bytes 3538952 | tf_op jit(solution)/shard_map/ppermute | solution.py:749
  64.6 1.9 collective-permute-start.14
  129.9 8.7 %copy-start.15 = (bf16[256,2304]{1,0:T(8,128)(2,1)S(1)}, bf16[256,2304]{1,0:T(8,128)(2,1)}, u32[]{:S(2)}) copy-start(bf16[256,2304]{1,0:T(8,128)(2,1)} %get-tuple-element.42.terms_ref) | copy-start | bytes 3538948
  141.3 10.6 %copy-start.4 = (bf16[256,2304]{1,0:T(8,128)(2,1)}, bf16[256,2304]{1,0:T(8,128)(2,1)S(1)}, u32[]{:S(2)}) copy-start(bf16[256,2304]{1,0:T(8,128)(2,1)S(1)} %add_terms.11.refs_1_) | copy-start | bytes 3538948
  141.3 39.0 %collective-permute-start.22 = (bf16[256,2304]{1,0:T(8,128)(2,1)S(1)}, bf16[256,2304]{1,0:T(8,128)(2,1)}, u32[]{:S(2)}, u32[]{:S(2)}) collective-permute-start(bf16[256,2304]{1,0:T(8,128)(2,1)S(1)} %add_terms.11.refs_1_), channel_id=1, source_target_pairs={{0,2},{4,0},{8,4},{12,8},{14,12},{10,14},{6,10},{2,6},{1,3},{5,1},... | collective-permute-start | bytes 3538952 | tf_op jit(solution)/shard_map/ppermute | solution.py:750
  145.7 42.8 %collective-permute-start.17 = (bf16[256,2304]{1,0:T(8,128)(2,1)}, bf16[256,2304]{1,0:T(8,128)(2,1)}, u32[]{:S(2)}, u32[]{:S(2)}) collective-permute-start(bf16[256,2304]{1,0:T(8,128)(2,1)} %add_terms.10.refs_0_), channel_id=1, source_target_pairs={{0,4},{4,8},{8,12},{12,14},{14,10},{10,6},{6,2},{2,0},{1,5},{5,9},... | collective-permute-start | bytes 3538952 | tf_op jit(solution)/shard_map/ppermute | solution.py:749
  146.8 29.0 %collective-permute-start.18 = (bf16[2,128,256]{2,1,0:T(8,128)(2,1)}, bf16[2,128,256]{2,1,0:T(8,128)(2,1)S(1)}, u32[]{:S(2)}, u32[]{:S(2)}) collective-permute-start(bf16[2,128,256]{2,1,0:T(8,128)(2,1)} %get-tuple-element.45), channel_id=1, source_target_pairs={{0,4},{2,6},{4,8},{6,10},{8,12},{10,14},{12,0},{14,2},{1,5},{3,7},... | collective-permute-start | bytes 393224 | tf_op jit(solution)/shard_map/ppermute | solution.py:625
  147.3 31.2 %collective-permute-start.19 = (bf16[2,128,256]{2,1,0:T(8,128)(2,1)}, bf16[2,128,256]{2,1,0:T(8,128)(2,1)S(1)}, u32[]{:S(2)}, u32[]{:S(2)}) collective-permute-start(bf16[2,128,256]{2,1,0:T(8,128)(2,1)} %get-tuple-element.46), channel_id=1, source_target_pairs={{0,8},{2,10},{4,12},{6,14},{8,0},{10,2},{12,4},{14,6},{1,9},{3,11}... | collective-permute-start | bytes 393224 | tf_op jit(solution)/shard_map/ppermute | solution.py:625
  149.9 30.4 %collective-permute-start.20 = (bf16[2,128,256]{2,1,0:T(8,128)(2,1)}, bf16[2,128,256]{2,1,0:T(8,128)(2,1)}, u32[]{:S(2)}, u32[]{:S(2)}) collective-permute-start(bf16[2,128,256]{2,1,0:T(8,128)(2,1)} %get-tuple-element.47), channel_id=1, source_target_pairs={{0,12},{2,14},{4,0},{6,2},{8,4},{10,6},{12,8},{14,10},{1,13},{3,15... | collective-permute-start | bytes 393224 | tf_op jit(solution)/shard_map/ppermute | solution.py:625
  162.5 26.0 %copy-start.5 = (bf16[256,2304]{1,0:T(8,128)(2,1)S(1)}, bf16[256,2304]{1,0:T(8,128)(2,1)}, u32[]{:S(2)}) copy-start(bf16[256,2304]{1,0:T(8,128)(2,1)} %get-tuple-element.44.terms_ref) | copy-start | bytes 3538948
  181.5 10.3 %copy-start.37 = (s32[2]{0:T(128)S(1)}, s32[2]{0:T(128)}, u32[]{:S(2)}) copy-start(s32[2]{0:T(128)} %compare_select_fusion.12) | copy-start | bytes 28
  181.5 10.5 %copy-start.29 = (s32[2]{0:T(128)S(1)}, s32[2]{0:T(128)}, u32[]{:S(2)}) copy-start(s32[2]{0:T(128)} %pad_add_fusion.1.place_ref) | copy-start | bytes 28
  184.6 19.5 %collective-permute-start.23 = (bf16[256,1280]{1,0:T(8,128)(2,1)}, bf16[256,1280]{1,0:T(8,128)(2,1)}, u32[]{:S(2)}, u32[]{:S(2)}) collective-permute-start(bf16[256,1280]{1,0:T(8,128)(2,1)} %add_terms.13.refs_5_), channel_id=1, source_target_pairs={{0,2},{4,0},{8,4},{12,8},{14,12},{10,14},{6,10},{2,6},{1,3},{5,1},... | collective-permute-start | bytes 1966088 | tf_op jit(solution)/shard_map/ppermute | solution.py:771
  191.7 18.6 %collective-permute-start.21 = (bf16[256,1280]{1,0:T(8,128)(2,1)}, bf16[256,1280]{1,0:T(8,128)(2,1)}, u32[]{:S(2)}, u32[]{:S(2)}) collective-permute-start(bf16[256,1280]{1,0:T(8,128)(2,1)} %add_terms.12.refs_4_), channel_id=1, source_target_pairs={{0,4},{4,8},{8,12},{12,14},{14,10},{10,6},{6,2},{2,0},{1,5},{5,9},... | collective-permute-start | bytes 1966088 | tf_op jit(solution)/shard_map/ppermute | solution.py:771
  195.5 14.8 %copy-start.3 = (bf16[256,2304]{1,0:T(8,128)(2,1)S(1)}, bf16[256,2304]{1,0:T(8,128)(2,1)}, u32[]{:S(2)}) copy-start(bf16[256,2304]{1,0:T(8,128)(2,1)} %get-tuple-element.43.terms_ref) | copy-start | bytes 3538948
  195.5 22.0 %collective-permute-start.25 = (bf16[256,1024]{1,0:T(8,128)(2,1)S(1)}, bf16[256,1024]{1,0:T(8,128)(2,1)S(1)}, u32[]{:S(2)}, u32[]{:S(2)}) collective-permute-start(bf16[256,1024]{1,0:T(8,128)(2,1)S(1)} %add_terms.15), channel_id=1, source_target_pairs={{0,2},{4,0},{8,4},{12,8},{14,12},{10,14},{6,10},{2,6},{1,3},{5,1},... | collective-permute-start | bytes 1572872 | tf_op jit(solution)/shard_map/ppermute | solution.py:772
  199.6 21.4 %collective-permute-start.24 = (bf16[256,1024]{1,0:T(8,128)(2,1)S(1)}, bf16[256,1024]{1,0:T(8,128)(2,1)S(1)}, u32[]{:S(2)}, u32[]{:S(2)}) collective-permute-start(bf16[256,1024]{1,0:T(8,128)(2,1)S(1)} %add_terms.14), channel_id=1, source_target_pairs={{0,4},{4,8},{8,12},{12,14},{14,10},{10,6},{6,2},{2,0},{1,5},{5,9},... | collective-permute-start | bytes 1572872 | tf_op jit(solution)/shard_map/ppermute | solution.py:772
  212.0 23.3 %collective-permute-start.26 = (bf16[2,256,256]{2,1,0:T(8,128)(2,1)S(1)}, bf16[2,256,256]{2,1,0:T(8,128)(2,1)S(1)}, u32[]{:S(2)}, u32[]{:S(2)}) collective-permute-start(bf16[2,256,256]{2,1,0:T(8,128)(2,1)S(1)} %get-tuple-element.52), channel_id=1, source_target_pairs={{0,12},{4,14},{8,10},{12,6},{14,2},{10,0},{6,4},{2,8},{1,13},{5,15... | collective-permute-start | bytes 786440 | tf_op jit(solution)/shard_map/ppermute | solution.py:782
  214.0 20.7 %collective-permute-start.31 = (bf16[128,256]{1,0:T(8,128)(2,1)S(1)}, bf16[128,256]{1,0:T(8,128)(2,1)S(1)}, u32[]{:S(2)}, u32[]{:S(2)}) collective-permute-start(bf16[128,256]{1,0:T(8,128)(2,1)S(1)} %get-tuple-element.50.refs_1_), channel_id=1, source_target_pairs={{0,2},{2,0},{4,6},{6,4},{8,10},{10,8},{12,14},{14,12},{1,3},{3,1},... | collective-permute-start | bytes 196616 | tf_op jit(solution)/shard_map/ppermute | solution.py:621
  214.2 22.5 %collective-permute-start.27 = (bf16[2,256,256]{2,1,0:T(8,128)(2,1)S(1)}, bf16[2,256,256]{2,1,0:T(8,128)(2,1)S(1)}, u32[]{:S(2)}, u32[]{:S(2)}) collective-permute-start(bf16[2,256,256]{2,1,0:T(8,128)(2,1)S(1)} %get-tuple-element.53), channel_id=1, source_target_pairs={{0,6},{4,2},{8,0},{12,4},{14,8},{10,12},{6,14},{2,10},{1,7},{5,3},... | collective-permute-start | bytes 786440 | tf_op jit(solution)/shard_map/ppermute | solution.py:782
  221.0 14.4 %copy-start.25 = (f32[512,128]{1,0:T(8,128)S(1)}, f32[512,128]{1,0:T(8,128)}, u32[]{:S(2)}) copy-start(f32[512,128]{1,0:T(8,128)} %get-tuple-element.40.solved_ref) | copy-start | bytes 786436
  221.0 14.4 %copy-start.28 = (f32[128,128]{1,0:T(8,128)S(1)}, f32[128,128]{1,0:T(8,128)}, u32[]{:S(2)}) copy-start(f32[128,128]{1,0:T(8,128)} %get-tuple-element.56.first_ref) | copy-start | bytes 196612
  221.4 15.4 %collective-permute-start.28 = (bf16[2,256,256]{2,1,0:T(8,128)(2,1)S(1)}, bf16[2,256,256]{2,1,0:T(8,128)(2,1)S(1)}, u32[]{:S(2)}, u32[]{:S(2)}) collective-permute-start(bf16[2,256,256]{2,1,0:T(8,128)(2,1)S(1)} %get-tuple-element.54), channel_id=1, source_target_pairs={{0,2},{4,0},{8,4},{12,8},{14,12},{10,14},{6,10},{2,6},{1,3},{5,1},... | collective-permute-start | bytes 786440 | tf_op jit(solution)/shard_map/ppermute | solution.py:782
  231.6 12.8 %collective-permute-start.29 = (bf16[1,256,256]{2,1,0:T(8,128)(2,1)S(1)}, bf16[1,256,256]{2,1,0:T(8,128)(2,1)S(1)}, u32[]{:S(2)}, u32[]{:S(2)}) collective-permute-start(bf16[1,256,256]{2,1,0:T(8,128)(2,1)S(1)} %get-tuple-element.55), channel_id=1, source_target_pairs={{0,14},{4,10},{8,6},{12,2},{14,0},{10,4},{6,8},{2,12},{1,15},{5,11... | collective-permute-start | bytes 393224 | tf_op jit(solution)/shard_map/ppermute | solution.py:782
  236.6 7.7 %collective-permute-start.32 = (f32[64,128]{1,0:T(8,128)S(1)}, f32[64,128]{1,0:T(8,128)S(1)}, u32[]{:S(2)}, u32[]{:S(2)}) collective-permute-start(f32[64,128]{1,0:T(8,128)S(1)} %slice_select_fusion), channel_id=1, source_target_pairs={{0,8},{2,10},{4,12},{6,14},{8,0},{10,2},{12,4},{14,6},{1,9},{3,11}... | collective-permute-start | bytes 98312 | tf_op jit(solution)/shard_map/ppermute | solution.py:796
  244.3 3.8 %collective-permute-start.33 = (f32[32,128]{1,0:T(8,128)S(1)}, f32[32,128]{1,0:T(8,128)S(1)}, u32[]{:S(2)}, u32[]{:S(2)}) collective-permute-start(f32[32,128]{1,0:T(8,128)S(1)} %slice_select_fusion.1), channel_id=1, source_target_pairs={{0,4},{2,6},{4,0},{6,2},{8,12},{10,14},{12,8},{14,10},{1,5},{3,7},... | collective-permute-start | bytes 49160 | tf_op jit(solution)/shard_map/ppermute | solution.py:796
  246.1 7.8 %collective-permute-start.30 = (bf16[8,256,256]{2,1,0:T(8,128)(2,1)}, bf16[8,256,256]{2,1,0:T(8,128)(2,1)S(1)}, u32[]{:S(2)}, u32[]{:S(2)}) collective-permute-start(bf16[8,256,256]{2,1,0:T(8,128)(2,1)} %for_sibling.1), channel_id=1, source_target_pairs={{0,1},{1,0},{2,3},{3,2},{4,5},{5,4},{6,7},{7,6},{8,9},{9,8},{10,11... | collective-permute-start | bytes 3145736 | tf_op jit(solution)/shard_map/ppermute | solution.py:789
  248.2 3.7 %collective-permute-start.34 = (f32[16,128]{1,0:T(8,128)S(1)}, f32[16,128]{1,0:T(8,128)S(1)}, u32[]{:S(2)}, u32[]{:S(2)}) collective-permute-start(f32[16,128]{1,0:T(8,128)S(1)} %slice_select_fusion.2), channel_id=1, source_target_pairs={{0,2},{2,0},{4,6},{6,4},{8,10},{10,8},{12,14},{14,12},{1,3},{3,1},... | collective-permute-start | bytes 24584 | tf_op jit(solution)/shard_map/ppermute | solution.py:796
  251.9 1.2 collective-permute-start.35
  (29 other events, 86.6 us)
